TPU v7x, 128 devices: a whole 4x4x4 slice. The times are simulated.
128 devices in a mesh: row: 8 (over x, core), col: 16 (over y, z).
Axes of the slice: x: 4, y: 4, z: 4, core: 2. Of those that a mesh axis runs over, the one named last changes fastest.
Arguments:
- images: bfloat16 [16384, 768], P(('row', 'col')), may hold values from -192 to 192
- texts: bfloat16 [16384, 768], P(('col', 'row')), may hold values from -192 to 192
- log_scale: float32 [], replicated, may hold values from 3 to 5.3
Outputs:
- grad_images: float32 [16384, 768], P(('row', 'col'))
- grad_texts: float32 [16384, 768], P(('col', 'row'))
- loss: float32 [], replicated
- grad_log_scale: float32 [], replicated
All inputs are finite; a program needn't handle non-finite values.
Results may differ from a plain program's by a relative error of at most 0.012.
The roundings to bfloat16 on the way count: a program that leaves them out, or rounds other values in their place, can miss the bound.
Values may be sent and summed in bfloat16 or wider, within the bound.
A program may use at most 64 MiB of HBM per device.

v0:
```python
import jax
import jax.numpy as jnp
from jax import lax
from jax.sharding import PartitionSpec as P

EPS = 1e-06


def unit_rows(values):
    full = values.astype(jnp.float32)
    inverse = lax.rsqrt(jnp.sum(full * full, axis=1, keepdims=True) + EPS)
    return (full * inverse, inverse)


def local(images, texts, log_scale):
    scale = jnp.exp(log_scale)
    image_unit, image_inv = unit_rows(images)
    text_unit, text_inv = unit_rows(texts)
    image_low = image_unit.astype(jnp.bfloat16)
    text_low = text_unit.astype(jnp.bfloat16)
    image_block = lax.all_gather(image_low, "col", axis=0, tiled=True)
    text_block = lax.all_gather(text_low, "row", axis=0, tiled=True)
    tile_rows = image_block.shape[0]
    tile_cols = text_block.shape[0]
    batch = tile_rows * lax.axis_size("row")
    logits = scale * jnp.dot(image_block, text_block.T, preferred_element_type=jnp.float32)
    row_peak = lax.pmax(jnp.max(logits, axis=1), "col")
    row_total = lax.psum(jnp.sum(jnp.exp(logits - row_peak[:, None]), axis=1), "col")
    col_peak = lax.pmax(jnp.max(logits, axis=0), "row")
    col_total = lax.psum(jnp.sum(jnp.exp(logits - col_peak[None, :]), axis=0), "row")
    row_lse = row_peak + jnp.log(row_total)
    col_lse = col_peak + jnp.log(col_total)
    row_ids = lax.axis_index("row") * tile_rows + jnp.arange(tile_rows, dtype=jnp.int32)
    col_ids = lax.axis_index("col") * tile_cols + jnp.arange(tile_cols, dtype=jnp.int32)
    onehot = (row_ids[:, None] == col_ids[None, :]).astype(jnp.float32)
    delta = (
        jnp.exp(logits - row_lse[:, None]) - onehot + (jnp.exp(logits - col_lse[None, :]) - onehot)
    ) / (2.0 * batch)
    delta_low = delta.astype(jnp.bfloat16)
    loss_part = jnp.sum(onehot * (row_lse[:, None] + col_lse[None, :] - 2.0 * logits))
    scale_part = jnp.sum(delta * logits)
    loss_sum, scale_sum = lax.psum((loss_part, scale_part), ("row", "col"))
    image_grad = lax.psum_scatter(
        scale * jnp.dot(delta_low, text_block, preferred_element_type=jnp.float32),
        "col",
        scatter_dimension=0,
        tiled=True,
    )
    grad_images = image_inv * (
        image_grad - image_unit * jnp.sum(image_unit * image_grad, axis=1, keepdims=True)
    )
    text_grad = lax.psum_scatter(
        scale
        * lax.dot_general(
            delta_low, image_block, (((0,), (0,)), ((), ())), preferred_element_type=jnp.float32
        ),
        "row",
        scatter_dimension=0,
        tiled=True,
    )
    grad_texts = text_inv * (
        text_grad - text_unit * jnp.sum(text_unit * text_grad, axis=1, keepdims=True)
    )
    return (grad_images, grad_texts, loss_sum / (2.0 * batch), scale_sum)


def solution(mesh):
    placed = (P(("row", "col"), None), P(("col", "row"), None), P())
    return jax.shard_map(
        local,
        mesh=mesh,
        in_specs=placed,
        out_specs=(P(("row", "col"), None), P(("col", "row"), None), P(), P()),
        check_vma=False,
    )
```

profile of v0, /device:TPU:0, one launch (start us, length us, event | category | flops | bytes accessed | tf_op | source)
XLA Modules:
  0.0 350.2 jit_solution(11311747145827549888)
XLA Ops:
  7.2 1.0 fusion.17
  8.3 1.7 fusion.6
  10.0 0.0 all-gather.3.cloned.1.call-start
  10.1 1.0 fusion.13
  11.1 1.7 fusion.9
  13.6 23.6 %all-gather.5.cloned.1.call-done = bf16[1024,768]{1,0:T(8,128)(2,1)} async-done(((bf16[128,768]{1,0:T(8,128)(2,1)}), bf16[1024,768]{1,0:T(8,128)(2,1)}) %all-gather.5.cloned.1.call-update) | async-done | bytes 1572880 | tf_op jit(solution)/shard_map/all_gather | solution.py:22
  37.2 51.1 %all-gather.3.cloned.1.call-done = bf16[2048,768]{1,0:T(8,128)(2,1)} async-done(((bf16[128,768]{1,0:T(8,128)(2,1)}), bf16[2048,768]{1,0:T(8,128)(2,1)}) %all-gather.3.cloned.1.call-update) | async-done | bytes 3145744 | tf_op jit(solution)/shard_map/all_gather | solution.py:21
  88.4 9.1 %multiply_reduce_fusion.2 = (f32[2048]{0:T(1024)S(1)}, f32[2048,1024]{1,0:T(8,128)}) fusion(f32[]{:T(128)S(6)} %exp.15, bf16[2048,768]{1,0:T(8,128)(2,1)} %all-gather.3.cloned.1.call-done, bf16[1024,768]{1,0:T(8,128)(2,1)} %all-gather.5.cloned.1.call-done), kind=kOutput, calls=%fused_computation.11 | convolution fusion | flops 3225417728 | bytes 13115396 | tf_op jit(solution)/shard_map/dot_general | solution.py:26
  97.4 38.6 %pmax.14 = f32[2048]{0:T(1024)S(1)} all-reduce(f32[2048]{0:T(1024)S(1)} %get-tuple-element.11), channel_id=1, replica_groups=mesh['row'=8,'col'=16] {'col'}, use_global_device_ids=true, to_apply=%region_3.0 | all-reduce | flops 2048 | bytes 16384 | tf_op jit(solution)/shard_map/pmax | solution.py:27
  136.1 4.5 %exponential_reduce_fusion.1 = (f32[2048]{0:T(1024)S(1)}, f32[1024]{0:T(1024)S(1)}) fusion(f32[2048,1024]{1,0:T(8,128)} %get-tuple-element.12, f32[2048]{0:T(1024)S(1)} %pmax.14, f32[]{:T(128)S(6)} %exp.15), kind=kLoop, calls=%fused_computation.8 | loop fusion | flops 8385536 | bytes 8409092 | tf_op jit(solution)/shard_map/reduce_sum | solution.py:28
  140.5 36.0 %psum.28 = f32[2048]{0:T(1024)S(1)} all-reduce(f32[2048]{0:T(1024)S(1)} %get-tuple-element.6), channel_id=1, replica_groups=mesh['row'=8,'col'=16] {'col'}, use_global_device_ids=true, to_apply=%region_5.0 | all-reduce | flops 2048 | bytes 16384 | tf_op jit(solution)/shard_map/psum | solution.py:28
  176.5 12.4 %pmax.15 = f32[1024]{0:T(1024)S(1)} all-reduce(f32[1024]{0:T(1024)S(1)} %get-tuple-element.7), channel_id=1, replica_groups=mesh['row'=8,'col'=16] {'row'}, use_global_device_ids=true, to_apply=%region_7.0 | all-reduce | flops 1024 | bytes 8192 | tf_op jit(solution)/shard_map/pmax | solution.py:29
  188.9 4.8 %exponential_reduce_fusion = f32[1024]{0:T(1024)S(1)} fusion(f32[2048,1024]{1,0:T(8,128)} %get-tuple-element.12, f32[1024]{0:T(1024)S(1)} %pmax.15, f32[]{:T(128)S(6)} %exp.15), kind=kLoop, calls=%fused_computation.7 | loop fusion | flops 6290432 | bytes 8396804 | tf_op jit(solution)/shard_map/reduce_sum | solution.py:30
  193.7 12.9 %psum.29 = f32[1024]{0:T(1024)S(1)} all-reduce(f32[1024]{0:T(1024)S(1)} %exponential_reduce_fusion), channel_id=1, replica_groups=mesh['row'=8,'col'=16] {'row'}, use_global_device_ids=true, to_apply=%region_9.0 | all-reduce | flops 1024 | bytes 8192 | tf_op jit(solution)/shard_map/psum | solution.py:30
  206.6 9.9 %multiply_reduce_fusion = (f32[]{:T(128)}, f32[]{:T(128)}, bf16[2048,1024]{1,0:T(8,128)(2,1)S(1)}) fusion(f32[2048,1024]{1,0:T(8,128)} %get-tuple-element.12, f32[1024]{0:T(1024)S(1)} %log_add_fusion.1, s32[1024]{0:T(1024)S(1)} %iota_add_fusion.1, f32[2048]{0:T(1024)S(1)} %log_add_fusion, f32[]{:T(128)S(6)} %exp.15, s32[2048]{0:T(1024)S(1)} %iota_add_fusion), kind=kLoop, calls=%fused_computation.6 | loop fusion | flops 35651584 | bytes 12607500 | tf_op jit(solution)/shard_map/reduce_sum | solution.py:41
  216.5 2.0 copy-done
  218.5 5.4 %convolution_multiply_fusion.1 = f32[1024,768]{1,0:T(8,128)} fusion(bf16[2048,1024]{1,0:T(8,128)(2,1)S(1)} %get-tuple-element.10, bf16[2048,768]{1,0:T(8,128)(2,1)S(1)} %copy-done.3, f32[]{:T(128)S(6)} %exp.15), kind=kOutput, calls=%fused_computation.13 | convolution fusion | flops 3222011904 | bytes 10485764 | tf_op jit(solution)/shard_map/dot_general | solution.py:54
  224.1 8.9 %convolution_multiply_fusion = f32[2048,768]{1,0:T(8,128)} fusion(bf16[2048,1024]{1,0:T(8,128)(2,1)} %copy-done, bf16[1024,768]{1,0:T(8,128)(2,1)} %all-gather.5.cloned.1.call-done, f32[]{:T(128)S(6)} %exp.15), kind=kOutput, calls=%fused_computation.12 | convolution fusion | flops 3222798336 | bytes 12058628 | tf_op jit(solution)/shard_map/dot_general | solution.py:44
  233.0 64.3 %all-reduce = (f32[]{:T(128)}, f32[]{:T(128)}) all-reduce(f32[]{:T(128)} %get-tuple-element.5, f32[]{:T(128)} %get-tuple-element.4), channel_id=1, replica_groups=mesh['row'=8,'col'=16] {'row','col'}, use_global_device_ids=true, to_apply=%region_15.0 | all-reduce | flops 2 | bytes 16 | tf_op jit(solution)/shard_map/psum | solution.py:42
  298.0 1.2 fusion.14
  299.2 1.9 fusion.16
  301.1 38.3 %reduce-scatter.3.cloned.1.call-done = f32[128,768]{1,0:T(8,128)} async-done(((f32[2048,768]{1,0:T(8,128)}), f32[128,768]{1,0:T(8,128)}) %reduce-scatter.3.cloned.1.call-update) | async-done | bytes 393232 | tf_op jit(solution)/shard_map/reduce_scatter | solution.py:43
  339.4 1.2 fusion.10
  340.6 1.9 fusion.12
  (21 shorter events, 0.3 us)
Async XLA Ops:
  7.2 30.1 %all-gather.5.cloned.1.call-start = ((), (), s32[]{:S(2)}) async-start(), calls=%async_computation.3 | async-start | bytes 1769472 | tf_op jit(solution)/shard_map/all_gather | solution.py:22
  10.0 78.4 %all-gather.3.cloned.1.call-start = ((), (), s32[]{:S(2)}) async-start(), calls=%async_computation.2 | async-start | bytes 3342336 | tf_op jit(solution)/shard_map/all_gather | solution.py:21
  12.8 285.1 %reduce-scatter.5.cloned.1.call-start = ((), (), s32[]{:S(2)}) async-start(), calls=%async_computation.5 | async-start | bytes 3538944 | tf_op jit(solution)/shard_map/reduce_scatter | solution.py:52
  193.7 24.8 %copy-start.3 = (bf16[2048,768]{1,0:T(8,128)(2,1)S(1)}, bf16[2048,768]{1,0:T(8,128)(2,1)}, u32[]{:S(2)}) copy-start(bf16[2048,768]{1,0:T(8,128)(2,1)} %all-gather.3.cloned.1.call-done) | copy-start | bytes 9437188
  216.5 2.0 copy-start
  224.0 74.0 %copy-start.1 = (bf16[128,768]{1,0:T(8,128)(2,1)S(1)}, bf16[128,768]{1,0:T(8,128)(2,1)}, u32[]{:S(2)}) copy-start(bf16[128,768]{1,0:T(8,128)(2,1)} %param.4) | copy-start | bytes 589828
  224.0 115.4 %copy-start.2 = (bf16[128,768]{1,0:T(8,128)(2,1)S(1)}, bf16[128,768]{1,0:T(8,128)(2,1)}, u32[]{:S(2)}) copy-start(bf16[128,768]{1,0:T(8,128)(2,1)} %param.3) | copy-start | bytes 589828
  224.0 115.4 %reduce-scatter.3.cloned.1.call-start = ((), (), s32[]{:S(2)}) async-start(), calls=%async_computation.4 | async-start | bytes 6684672 | tf_op jit(solution)/shard_map/reduce_scatter | solution.py:43
Sparse Core Ops, SparseCore 0:
  10.3 26.9 all-gather.4
  40.0 48.3 all-gather.2
  224.1 31.3 reduce-scatter.4
  258.8 80.5 reduce-scatter.2
where the time goes:
time: 351 us; the launch traced here: 350 us
  blocking collectives  164 us (47%)
  waiting for transfers between devices  113 us (32%)
  other arithmetic  30.9 us (9%)
  matrix products  23.4 us (7%)
  between operations  16.3 us (5%)
    psum x1, blocking collectives, local(): loss_sum, scale_sum = lax.psum((loss_part, scale_part), ('row', 'col'))  64.3 us
    all_gather x1, waiting for transfers between devices, local(): image_block = lax.all_gather(image_low, 'col', axis=0, tiled=True)  51.1 us
    pmax x1, blocking collectives, local(): row_peak = lax.pmax(jnp.max(logits, axis=1), 'col')  38.6 us
    reduce_scatter x1, waiting for transfers between devices, local(): lax.psum_scatter(scale * jnp.dot(delta_low, text_block, preferred_element...  38.3 us
    psum x1, blocking collectives, local(): lax.psum(jnp.sum(jnp.exp(logits - row_peak[:, None]), axis=1), 'col')  36 us
    all_gather x1, waiting for transfers between devices, local(): text_block = lax.all_gather(text_low, 'row', axis=0, tiled=True)  23.6 us
    psum x1, blocking collectives, local(): lax.psum(jnp.sum(jnp.exp(logits - col_peak[None, :]), axis=0), 'row')  12.9 us
    pmax x1, blocking collectives, local(): col_peak = lax.pmax(jnp.max(logits, axis=0), 'row')  12.4 us
  transfers between devices with their start and end apart: 4, of which 3 were waited for; matrix products, arithmetic and copies ran while one was open for 4% of the time, Pallas kernels for 0%

commit v1 on v0

v1 whole, which is shorter than its diff:
```python
import math

import jax
import jax.numpy as jnp
from jax import lax
from jax.experimental import pallas as pl
from jax.experimental.pallas import tpu as pltpu
from jax.sharding import PartitionSpec as P

EPS = 1e-06
LOG2E = math.log2(math.e)
LN2 = math.log(2.0)
MESH = pl.DeviceIdType.MESH
N = 4
R = 128
H = R // 2
E = 768
IMAGES = N * N * R
TEXTS = 2 * N * R
PAIRS = IMAGES // (2 * R)


def unit_rows(values):
    full = values.astype(jnp.float32)
    inverse = lax.rsqrt(jnp.sum(full * full, axis=1, keepdims=True) + EPS)
    return full * inverse, inverse


def lse2(values):
    peak = values[0]
    for v in values[1:]:
        peak = jnp.maximum(peak, v)
    total = jnp.exp2(values[0] - peak)
    for v in values[1:]:
        total = total + jnp.exp2(v - peak)
    return peak + jnp.log(total) * LOG2E


def project(values, grad):
    unit, inverse = unit_rows(values)
    return inverse * (grad - unit * jnp.sum(unit * grad, axis=1, keepdims=True))


def kernel(
    img_ref, txt_ref, scale_ref, gi_ref, gt_ref, loss_ref, gs_ref,
    img, txt, logit, delta, stage, own0, own1, a0, a1, sb0, sb1, b0, b1,
    tst, c0, sd, dd, rowl, rowy, rowz, coll, colc, colx, sums,
    ga_s, gb_s, g_r, tx_s, tc_s, t_r, ry_s, ry_r, rz_s, rz_r, cc_s, cc_r, cx_s, cx_r,
    pa_s, pa0_r, pa1_r, pb_s, pb_r, qc_s, qc_r, qx_s, qx_r, su_s, su_r,
):
    row, col = lax.axis_index("row"), lax.axis_index("col")
    x, c = row // 2, row % 2
    y, z = col // N, col % N
    sib = (row + 1 - 2 * c, col)

    def at_x(v):
        return (v * 2 + c, col)

    def at_y(v):
        return (row, v * N + z)

    def at_z(v):
        return (row, y * N + v)

    def turn(v, d):
        return lax.rem(v + d, N)

    def send(src, dst, ssem, rsem, dev):
        return pltpu.make_async_remote_copy(
            src_ref=src, dst_ref=dst, send_sem=ssem, recv_sem=rsem, device_id=dev, device_id_type=MESH
        )

    barrier = pltpu.get_barrier_semaphore()
    for d in range(1, N):
        for dev in (at_x(turn(x, d)), at_y(turn(y, d)), at_z(turn(z, d))):
            pl.semaphore_signal(barrier, inc=1, device_id=dev, device_id_type=MESH)
    pl.semaphore_signal(barrier, inc=1, device_id=sib, device_id_type=MESH)

    def block(k):
        return pl.ds(pl.multiple_of(k * R, R), R)

    def half(k, h):
        return pl.ds(pl.multiple_of(k * R + h * H, H), H)

    mine = c * N + x
    img[block(col), :] = unit_rows(img_ref[...])[0].astype(jnp.bfloat16)
    txt[block(mine), :] = unit_rows(txt_ref[...])[0].astype(jnp.bfloat16)
    scale = jnp.exp(jnp.full((1, 1), scale_ref[0], jnp.float32))
    scale2 = scale * LOG2E
    pl.semaphore_wait(barrier, 3 * (N - 1) + 1)

    def image_copy(k, h, ssem, dev):
        view = img.at[half(k, h), :]
        return send(view, view, ssem, g_r.at[k, h], dev)

    def text_copy(slot, ssem, dev):
        view = txt.at[block(slot), :]
        return send(view, view, ssem, t_r.at[slot], dev)

    first = []
    for d in range(1, N):
        first.append(image_copy(col, 0, ga_s.at[0, d], at_y(turn(y, d))))
        first.append(image_copy(col, 1, ga_s.at[1, d], at_z(turn(z, d))))
        first.append(text_copy(mine, tx_s.at[d], at_x(turn(x, d))))
    first.append(text_copy(mine, tc_s.at[0], sib))
    for d in range(1, N):
        first.append(image_copy(col, 0, gb_s.at[0, 0, d], at_z(turn(z, d))))
        first.append(image_copy(col, 1, gb_s.at[1, 0, d], at_y(turn(y, d))))
    for copy in first:
        copy.start()
    for d in (1, 3, 2):
        ky = turn(y, d) * N + z
        image_copy(ky, 0, ga_s.at[0, d], at_y(y)).wait_recv()
        for e in range(1, N):
            copy = image_copy(ky, 0, gb_s.at[0, d, e], at_z(turn(z, e)))
            copy.start()
            first.append(copy)
        kz = y * N + turn(z, d)
        image_copy(kz, 1, ga_s.at[1, d], at_z(z)).wait_recv()
        for e in range(1, N):
            copy = image_copy(kz, 1, gb_s.at[1, d, e], at_y(turn(y, e)))
            copy.start()
            first.append(copy)
        slot = c * N + turn(x, d)
        text_copy(slot, tx_s.at[d], sib).wait_recv()
        copy = text_copy(slot, tc_s.at[d], sib)
        copy.start()
        first.append(copy)
    for d in range(N):
        text_copy((1 - c) * N + turn(x, d), tc_s.at[d], sib).wait_recv()

    def tile_step(i, carry):
        p = lax.rem(col // 2 + i, PAIRS)
        for b in range(2):
            k = 2 * p + b

            @pl.when(k % N != z)
            def _():
                image_copy(k, 0, ga_s.at[0, 0], sib).wait_recv()

            @pl.when(k // N != y)
            def _():
                image_copy(k, 1, ga_s.at[0, 0], sib).wait_recv()

        rows = pl.ds(pl.multiple_of(p * 2 * R, 2 * R), 2 * R)
        l = scale2 * lax.dot_general(
            img[rows, :], txt[...], (((1,), (1,)), ((), ())), preferred_element_type=jnp.float32
        )
        logit[rows, :] = l
        rmax = jnp.max(l, axis=1, keepdims=True)
        cmax = jnp.max(l, axis=0, keepdims=True)
        rsum = jnp.sum(jnp.exp2(l - rmax), axis=1, keepdims=True)
        csum = jnp.sum(jnp.exp2(l - cmax), axis=0, keepdims=True)
        rlse = rmax + jnp.log(rsum) * LOG2E
        rowl[p] = jnp.broadcast_to(rlse, (2 * R, R)).T[:1, :]
        coll[p] = cmax + jnp.log(csum) * LOG2E
        return carry

    lax.fori_loop(0, PAIRS, tile_step, 0)

    rowy[y] = rowl[...]
    rowc = []
    for d in range(1, N):
        copy = send(rowy.at[y], rowy.at[y], ry_s.at[d], ry_r.at[y], at_y(turn(y, d)))
        copy.start()
        rowc.append(copy)
    colc[c] = lse2([coll[p] for p in range(PAIRS)])
    copy = send(colc.at[c], colc.at[c], cc_s.at[0], cc_r.at[c], sib)
    copy.start()
    rowc.append(copy)
    send(colc.at[1 - c], colc.at[1 - c], cc_s.at[0], cc_r.at[1 - c], sib).wait_recv()
    colx[x] = lse2([colc[0], colc[1]])
    for d in range(1, N):
        copy = send(colx.at[x], colx.at[x], cx_s.at[d], cx_r.at[x], at_x(turn(x, d)))
        copy.start()
        rowc.append(copy)
    for d in range(1, N):
        t = turn(y, d)
        send(rowy.at[t], rowy.at[t], ry_s.at[d], ry_r.at[t], sib).wait_recv()
    rowz[z] = lse2([rowy[v] for v in range(N)])
    for d in range(1, N):
        copy = send(rowz.at[z], rowz.at[z], rz_s.at[d], rz_r.at[z], at_z(turn(z, d)))
        copy.start()
        rowc.append(copy)
    for d in range(1, N):
        t = turn(x, d)
        send(colx.at[t], colx.at[t], cx_s.at[d], cx_r.at[t], sib).wait_recv()
    clse = lse2([colx[v] for v in range(N)])
    for d in range(1, N):
        t = turn(z, d)
        send(rowz.at[t], rowz.at[t], rz_s.at[d], rz_r.at[t], sib).wait_recv()
    rowl[...] = lse2([rowz[v] for v in range(N)])
    coll[0] = clse

    lane = lax.broadcasted_iota(jnp.int32, (8, R), 1)
    eye = lax.broadcasted_iota(jnp.int32, (R, R), 0) == lax.broadcasted_iota(jnp.int32, (R, R), 1)

    def a0_copy(k, dev):
        ky, kz = k // N, k % N
        return send(stage.at[half(k, 0), :], a0.at[y, kz], pa_s.at[k, 0], pa0_r.at[y, kz], (row, ky * N + z))

    def a1_copy(k, dev):
        ky, kz = k // N, k % N
        return send(stage.at[half(k, 1), :], a1.at[z, ky], pa_s.at[k, 1], pa1_r.at[z, ky], (row, y * N + kz))

    sums[0, c] = jnp.zeros((8, R), jnp.float32)

    def grad_step(i, total):
        p = lax.rem(2 * y + 2 + i, PAIRS)
        rows = pl.ds(pl.multiple_of(p * 2 * R, 2 * R), 2 * R)
        l = logit[rows, :]
        rcol = jnp.broadcast_to(rowl[p], (R, 2 * R)).T[:, :1]
        d = jnp.exp2(l - rcol) + jnp.exp2(l - coll[0])
        total = total + jnp.sum(d * l, axis=0, keepdims=True)
        delta[rows, :] = d.astype(jnp.bfloat16)
        for b in range(2):
            k = 2 * p + b
            j = row * (N * N) + k - col * (2 * N)

            @pl.when(jnp.logical_and(j >= 0, j < 2 * N))
            def _():
                cols = block((j % 2) * N + j // 2)
                sub = logit[block(k), cols]
                one = eye.astype(jnp.float32)
                rc = jnp.broadcast_to(rowl[p][:, b * R : (b + 1) * R], (R, R)).T[:, :1]
                cc = coll[0, :, cols]
                fixed = (jnp.exp2(sub - rc) - one) + (jnp.exp2(sub - cc) - one)
                delta[block(k), cols] = fixed.astype(jnp.bfloat16)
                lossp = jnp.sum(jnp.where(eye, rc + cc - 2.0 * sub, 0.0), axis=0, keepdims=True)
                lossp = jnp.sum(lossp, axis=1, keepdims=True)
                diag = jnp.sum(jnp.where(eye, -2.0 * sub, 0.0), axis=0, keepdims=True)
                diag = jnp.sum(diag, axis=1, keepdims=True)
                sums[0, c] = sums[0, c] + jnp.where(lane == 0, lossp, jnp.where(lane == 1, diag, 0.0))

        part = jnp.dot(delta[rows, :], txt[...], preferred_element_type=jnp.float32)
        stage[rows, :] = part.astype(jnp.bfloat16)
        for b in range(2):
            k = 2 * p + b
            ky, kz = k // N, k % N

            @pl.when(ky != y)
            def _():
                a0_copy(k, None).start()

            @pl.when(ky == y)
            def _():
                own0[kz] = part[b * R : b * R + H, :]

            @pl.when(kz != z)
            def _():
                a1_copy(k, None).start()

            @pl.when(kz == z)
            def _():
                own1[ky] = part[b * R + H : (b + 1) * R, :]

        return total

    total = lax.fori_loop(0, PAIRS, grad_step, jnp.zeros((1, TEXTS), jnp.float32))
    total = jnp.sum(total, axis=1, keepdims=True)
    sums[0, c] = sums[0, c] + jnp.where(lane == 1, total, 0.0)

    def sum_copies(level, at, where, count):
        return [
            send(sums.at[level, at], sums.at[level, at], su_s.at[level, d], su_r.at[level, at], where(d))
            for d in range(1, count)
        ]

    def sum_wait(level, at):
        send(sums.at[level, at], sums.at[level, at], su_s.at[level, 0], su_r.at[level, at], sib).wait_recv()

    copies = sum_copies(0, c, lambda d: sib, 2)
    copies[0].start()
    rowc += copies

    other = pl.ds(pl.multiple_of((1 - c) * N * R, N * R), N * R)
    ours = pl.ds(pl.multiple_of(c * N * R, N * R), N * R)
    tst[...] = lax.dot_general(
        delta[:, other], img[...], (((0,), (0,)), ((), ())), preferred_element_type=jnp.float32
    ).astype(jnp.bfloat16)
    for v in range(N):
        copy = send(tst.at[pl.ds(v * R, R), :], c0.at[v], qc_s.at[v], qc_r.at[v], sib)
        copy.start()
        rowc.append(copy)
    sum_wait(0, 1 - c)
    sums[1, x] = sums[0, 0] + sums[0, 1]
    copies = sum_copies(1, x, lambda d: at_x(turn(x, d)), N)
    for copy in copies:
        copy.start()
    rowc += copies
    qown = lax.dot_general(
        delta[:, ours], img[...], (((0,), (0,)), ((), ())), preferred_element_type=jnp.float32
    )
    for v in range(N):
        send(c0.at[v], c0.at[v], qc_s.at[v], qc_r.at[v], sib).wait_recv()
        sd[v] = qown[v * R : (v + 1) * R, :] + c0[v].astype(jnp.float32)
        dd[N + v] = sd[v].astype(jnp.bfloat16)
    for d in range(1, N):
        t = turn(x, d)
        copy = send(dd.at[N + t], dd.at[x], qx_s.at[d], qx_r.at[x], at_x(t))
        copy.start()
        rowc.append(copy)
    for d in range(1, N):
        sum_wait(1, turn(x, d))
    sums[2, y] = sums[1, 0] + sums[1, 1] + sums[1, 2] + sums[1, 3]
    copies = sum_copies(2, y, lambda d: at_y(turn(y, d)), N)
    for copy in copies:
        copy.start()
    rowc += copies

    for d in (1, 2, 3, 0):
        t = turn(z, d)
        acc = own0[t]
        for e in range(1, N):
            s = turn(y, e)
            send(a0.at[s, t], a0.at[s, t], pa_s.at[0, 0], pa0_r.at[s, t], sib).wait_recv()
            acc = acc + a0[s, t].astype(jnp.float32)
        own0[t] = acc
        if d:
            sb0[d] = acc.astype(jnp.bfloat16)
            copy = send(sb0.at[d], b0.at[z], pb_s.at[0, d], pb_r.at[0, z], at_z(t))
            copy.start()
            rowc.append(copy)
        t = turn(y, d)
        acc = own1[t]
        for e in range(1, N):
            s = turn(z, e)
            send(a1.at[s, t], a1.at[s, t], pa_s.at[0, 0], pa1_r.at[s, t], sib).wait_recv()
            acc = acc + a1[s, t].astype(jnp.float32)
        own1[t] = acc
        if d:
            sb1[d] = acc.astype(jnp.bfloat16)
            copy = send(sb1.at[d], b1.at[y], pb_s.at[1, d], pb_r.at[1, y], at_y(t))
            copy.start()
            rowc.append(copy)
    for d in range(1, N):
        sum_wait(2, turn(y, d))
    sums[3, z] = sums[2, 0] + sums[2, 1] + sums[2, 2] + sums[2, 3]
    copies = sum_copies(3, z, lambda d: at_z(turn(z, d)), N)
    for copy in copies:
        copy.start()
    rowc += copies

    factor = scale * (1.0 / (2.0 * TEXTS * N * N))
    acc = sd[x]
    for d in range(1, N):
        t = turn(x, d)
        send(dd.at[t], dd.at[t], qx_s.at[d], qx_r.at[t], sib).wait_recv()
        acc = acc + dd[t].astype(jnp.float32)
    gt_ref[...] = project(txt_ref[...], factor * acc)
    acc = own0[z]
    for d in range(1, N):
        t = turn(z, d)
        send(b0.at[t], b0.at[t], pb_s.at[0, d], pb_r.at[0, t], sib).wait_recv()
        acc = acc + b0[t].astype(jnp.float32)
    gi_ref[:H, :] = project(img_ref[:H, :], factor * acc)
    acc = own1[y]
    for d in range(1, N):
        t = turn(y, d)
        send(b1.at[t], b1.at[t], pb_s.at[1, d], pb_r.at[1, t], sib).wait_recv()
        acc = acc + b1[t].astype(jnp.float32)
    gi_ref[H:, :] = project(img_ref[H:, :], factor * acc)
    for d in range(1, N):
        sum_wait(3, turn(z, d))
    whole = (sums[3, 0] + sums[3, 1] + sums[3, 2] + sums[3, 3]) * (LN2 / (2.0 * TEXTS * N * N))
    top = lax.broadcasted_iota(jnp.int32, (8, R), 0) == 0
    loss_ref[0] = jnp.sum(jnp.where(jnp.logical_and(top, lane == 0), whole, 0.0))
    gs_ref[0] = jnp.sum(jnp.where(jnp.logical_and(top, lane == 1), whole, 0.0))

    for copy in first + rowc:
        copy.wait_send()

    def drain(k, carry):
        @pl.when(k // N != y)
        def _():
            a0_copy(k, None).wait_send()

        @pl.when(k % N != z)
        def _():
            a1_copy(k, None).wait_send()

        return carry

    lax.fori_loop(0, N * N, drain, 0)


def local(images, texts, log_scale):
    f32, bf16 = jnp.float32, jnp.bfloat16
    dma = pltpu.SemaphoreType.DMA
    vmem = pl.BlockSpec(memory_space=pltpu.VMEM)
    smem = pl.BlockSpec(memory_space=pltpu.SMEM)
    gi, gt, loss, gs = pl.pallas_call(
        kernel,
        out_shape=(
            jax.ShapeDtypeStruct((R, E), f32),
            jax.ShapeDtypeStruct((R, E), f32),
            jax.ShapeDtypeStruct((1,), f32),
            jax.ShapeDtypeStruct((1,), f32),
        ),
        in_specs=[vmem, vmem, smem],
        out_specs=(vmem, vmem, smem, smem),
        scratch_shapes=[
            pltpu.VMEM((IMAGES, E), bf16),
            pltpu.VMEM((TEXTS, E), bf16),
            pltpu.VMEM((IMAGES, TEXTS), f32),
            pltpu.VMEM((IMAGES, TEXTS), bf16),
            pltpu.VMEM((IMAGES, E), bf16),
            pltpu.VMEM((N, H, E), f32),
            pltpu.VMEM((N, H, E), f32),
            pltpu.VMEM((N, N, H, E), bf16),
            pltpu.VMEM((N, N, H, E), bf16),
            pltpu.VMEM((N, H, E), bf16),
            pltpu.VMEM((N, H, E), bf16),
            pltpu.VMEM((N, H, E), bf16),
            pltpu.VMEM((N, H, E), bf16),
            pltpu.VMEM((N * R, E), bf16),
            pltpu.VMEM((N, R, E), bf16),
            pltpu.VMEM((N, R, E), f32),
            pltpu.VMEM((2 * N, R, E), bf16),
            pltpu.VMEM((PAIRS, 1, 2 * R), f32),
            pltpu.VMEM((N, PAIRS, 1, 2 * R), f32),
            pltpu.VMEM((N, PAIRS, 1, 2 * R), f32),
            pltpu.VMEM((PAIRS, 1, TEXTS), f32),
            pltpu.VMEM((2, 1, TEXTS), f32),
            pltpu.VMEM((N, 1, TEXTS), f32),
            pltpu.VMEM((4, N, 8, R), f32),
            dma((2, N)),
            dma((2, N, N)),
            dma((N * N, 2)),
            dma((N,)),
            dma((N,)),
            dma((2 * N,)),
            dma((N,)), dma((N,)), dma((N,)), dma((N,)),
            dma((1,)), dma((2,)), dma((N,)), dma((N,)),
            dma((N * N, 2)), dma((N, N)), dma((N, N)),
            dma((2, N)), dma((2, N)),
            dma((N,)), dma((N,)), dma((N,)), dma((N,)),
            dma((4, N)), dma((4, N)),
        ],
        compiler_params=pltpu.CompilerParams(
            collective_id=0, has_side_effects=True, vmem_limit_bytes=56 * 1024 * 1024
        ),
    )(images, texts, log_scale.reshape(1))
    return gi, gt, loss.reshape(()), gs.reshape(())


def solution(mesh):
    placed = (P(("row", "col"), None), P(("col", "row"), None), P())
    return jax.shard_map(
        local,
        mesh=mesh,
        in_specs=placed,
        out_specs=(P(("row", "col"), None), P(("col", "row"), None), P(), P()),
        check_vma=False,
    )
```

time: 351 us -> 82.1 us (0.23)
  blocking collectives: 164 us -> 0 us
  waiting for transfers between devices: 113 us -> 0 us
  Pallas kernels: 0 us -> 73.2 us
  other arithmetic: 30.9 us -> 0 us
  matrix products: 23.4 us -> 0 us
  between operations: 16.3 us -> 4.81 us
    psum x3 -> x0, blocking collectives: 113 us -> none  [the longest x1 64.3 us: local(): loss_sum, scale_sum = lax.psum((loss_part, scale_part), ('row', 'col'))]
    all_gather x2 -> x0, waiting for transfers between devices: 74.8 us -> none  [the longest x1 51.1 us: local(): image_block = lax.all_gather(image_low, 'col', axis=0, tiled=True)]
    pallas_call x0 -> x1, Pallas kernels: none -> 73.2 us  [local(): pl.pallas_call(kernel, out_shape=(jax.ShapeDtypeStruct((R, E), f32), jax....]
    pmax x2 -> x0, blocking collectives: 51 us -> none  [the longest x1 38.6 us: local(): row_peak = lax.pmax(jnp.max(logits, axis=1), 'col')]
    reduce_scatter x2 -> x0, waiting for transfers between devices: 38.3 us -> none  [the longest x1 38.3 us: local(): lax.psum_scatter(scale * jnp.dot(delta_low, text_block, preferred_element...]
    reduce_sum x7 -> x0, other arithmetic: 23.6 us -> none  [the longest x1 9.87 us: local(): scale_part = jnp.sum(delta * logits)]
    dot_general x3 -> x0, matrix products: 23.4 us -> none  [the longest x1 9.06 us: local(): jnp.dot(image_block, text_block.T, preferred_element_type=jnp.float32)]
    mul x2 -> x0, other arithmetic: 3.85 us -> none  [the longest x1 1.92 us: local(): text_inv * (text_grad - text_unit * jnp.sum(text_unit * text_grad, axis=1...]
  transfers between devices with their start and end apart: 4 -> 0, of which waited for: 3 -> 0; matrix products, arithmetic and copies ran while one was open for 4% -> 0% of each run, Pallas kernels for 0% -> 0%
where the time goes in v1:
time: 82.1 us; the launch traced here: 80.6 us
  Pallas kernels  73.2 us (89%)
  between operations  4.81 us (6%)
  local copies, waits for them, and re-layouts  2.57 us (3%)
    pallas_call x1, Pallas kernels, local(): pl.pallas_call(kernel, out_shape=(jax.ShapeDtypeStruct((R, E), f32), jax....  73.2 us
    unnamed x4, local copies, waits for them, and re-layouts  2.57 us

profile of v1, /device:TPU:0, one launch (start us, length us, event | category | flops | bytes accessed | tf_op | source)
XLA Modules:
  0.0 80.6 jit_solution(18375679916263857329)
XLA Ops:
  1.3 73.2 %shard_map.66 = (f32[128,768]{1,0:T(8,128)}, f32[128,768]{1,0:T(8,128)}, f32[1]{0:T(128)}, f32[1]{0:T(128)}) custom-call(bf16[128,768]{1,0:T(8,128)(2,1)} %img_ref.1, bf16[128,768]{1,0:T(8,128)(2,1)} %txt_ref.1, f32[1]{0:T(128)} %bitcast.3.scale_ref), custom_call_target="tpu_custom_call" | custom-call | tf_op jit(solution)/shard_map/pallas_call | solution.py:392
  74.5 0.0 copy-start
  74.5 1.8 %copy.12 = f32[128,768]{1,0:T(8,128)} copy(f32[128,768]{1,0:T(8,128)} %get-tuple-element.16) | data formatting | bytes 786432
  76.3 0.0 copy-done
  76.3 0.7 copy.13
Async XLA Ops:
  74.5 1.8 %copy-start = (f32[128,768]{1,0:T(8,128)S(1)}, f32[128,768]{1,0:T(8,128)}, u32[]{:S(2)}) copy-start(f32[128,768]{1,0:T(8,128)} %get-tuple-element.17) | copy-start | bytes 1179652

commit v2 on v0

v2 whole, which is shorter than its diff:
```python
import math

import jax
import jax.numpy as jnp
from jax import lax
from jax.experimental import pallas as pl
from jax.experimental.pallas import tpu as pltpu
from jax.sharding import PartitionSpec as P

EPS = 1e-06
LOG2E = math.log2(math.e)
LN2 = math.log(2.0)
MESH = pl.DeviceIdType.MESH
N = 4
R = 128
H = R // 2
E = 768
IMAGES = N * N * R
TEXTS = 2 * N * R
PAIRS = IMAGES // (2 * R)


def unit_rows(values):
    full = values.astype(jnp.float32)
    inverse = lax.rsqrt(jnp.sum(full * full, axis=1, keepdims=True) + EPS)
    return full * inverse, inverse


def lse2(values):
    peak = values[0]
    for v in values[1:]:
        peak = jnp.maximum(peak, v)
    total = jnp.exp2(values[0] - peak)
    for v in values[1:]:
        total = total + jnp.exp2(v - peak)
    return peak + jnp.log(total) * LOG2E


def project(values, grad):
    unit, inverse = unit_rows(values)
    return inverse * (grad - unit * jnp.sum(unit * grad, axis=1, keepdims=True))


def kernel(
    img_ref, txt_ref, scale_ref, gi_ref, gt_ref, loss_ref, gs_ref,
    img, txt, logit, delta, stage_s, stage_c, stage_i, stage_t,
    own0, own1, a0, a1, sb, b0, b1,
    rowl, rowp, rowx, coll, colp, colz, sums,
    g_s, g_r, t_r, rp_r, rx_r, cp_r, cz_r, qc_s, qc_r, pa0_s, pa1_s, pa0_r, pa1_r, pb0_r, pb1_r, su_r,
):
    row, col = lax.axis_index("row"), lax.axis_index("col")
    x, c = row // 2, row % 2
    y, z = col // N, col % N
    yb, yo = y % 2, y // 2
    yi = y + 1 - 2 * yb
    yt = N - 1 - y
    sib = (row + 1 - 2 * c, col)
    by_i = (row, yi * N + z)
    by_t = (row, yt * N + z)
    by_is = (row + 1 - 2 * c, yi * N + z)

    def at_x(v):
        return (v * 2 + c, col)

    def at_z(v):
        return (row, y * N + v)

    def turn(v, d):
        return lax.rem(v + d, N)

    def send(src, dst, ssem, rsem, dev):
        return pltpu.make_async_remote_copy(
            src_ref=src, dst_ref=dst, send_sem=ssem, recv_sem=rsem, device_id=dev, device_id_type=MESH
        )

    started = []

    def go(src, dst, rsem, dev):
        copy = send(src, dst, g_s.at[len(started)], rsem, dev)
        copy.start()
        started.append(copy)

    def take(dst, rsem):
        send(dst, dst, g_s.at[0], rsem, sib).wait_recv()

    barrier = pltpu.get_barrier_semaphore()
    peers = [by_i, by_t, by_is, sib]
    for d in range(1, N):
        peers += [at_x(turn(x, d)), at_z(turn(z, d))]
    for dev in peers:
        pl.semaphore_signal(barrier, inc=1, device_id=dev, device_id_type=MESH)

    def block(k):
        return pl.ds(pl.multiple_of(k * R, R), R)

    def pair(p):
        return pl.ds(pl.multiple_of(p * 2 * R, 2 * R), 2 * R)

    def half(k, h):
        return pl.ds(pl.multiple_of(k * R + h * H, H), H)

    def islot(cc, b, xx):
        return cc * 2 * N + b * N + xx

    def tslot(o, zz):
        return o * N + zz

    imine, tmine = islot(c, yb, x), tslot(yo, z)
    img[block(imine), :] = unit_rows(img_ref[...])[0].astype(jnp.bfloat16)
    txt[block(tmine), :] = unit_rows(txt_ref[...])[0].astype(jnp.bfloat16)
    scale = jnp.exp(jnp.full((1, 1), scale_ref[0], jnp.float32))
    scale2 = scale * LOG2E
    pl.semaphore_wait(barrier, len(peers))

    def iview(k, h):
        return img.at[half(k, h), :]

    def tview(k, h):
        return txt.at[half(k, h), :]

    def igo(k, h, dev):
        go(iview(k, h), iview(k, h), g_r.at[k, h], dev)

    def tgo(k, h, dev):
        go(tview(k, h), tview(k, h), t_r.at[k, h], dev)

    def itake(k, h):
        take(iview(k, h), g_r.at[k, h])

    def ttake(k, h):
        take(tview(k, h), t_r.at[k, h])

    igo(imine, 0, by_i)
    tgo(tmine, 0, by_t)
    for h in (1, 0):
        for d in range(1, N):
            igo(imine, h, at_x(turn(x, d)))
            tgo(tmine, h, at_z(turn(z, d)))
    igo(imine, 1, by_i)
    tgo(tmine, 1, by_t)
    for h in range(2):
        igo(imine, h, sib)
    k = islot(c, 1 - yb, x)
    itake(k, 0)
    for d in range(1, N):
        igo(k, 0, at_x(turn(x, d)))
    t = tslot(1 - yo, z)
    ttake(t, 0)
    for d in range(1, N):
        tgo(t, 0, at_z(turn(z, d)))
    igo(k, 0, sib)
    for d in (1, 3, 2):
        k = islot(c, yb, turn(x, d))
        itake(k, 1)
        igo(k, 1, by_i)
        igo(k, 1, sib)
        t = tslot(yo, turn(z, d))
        ttake(t, 1)
        tgo(t, 1, by_t)
    for d in (1, 3, 2):
        k = islot(c, yb, turn(x, d))
        itake(k, 0)
        igo(k, 0, sib)
    for d in (1, 3, 2):
        ttake(tslot(yo, turn(z, d)), 0)

    def tile(p, o):
        cols = pl.ds(pl.multiple_of(o * N * R, N * R), N * R)
        l = scale2 * lax.dot_general(
            img[pair(p), :], txt[cols, :], (((1,), (1,)), ((), ())), preferred_element_type=jnp.float32
        )
        logit[pair(p), cols] = l
        rmax = jnp.max(l, axis=1, keepdims=True)
        cmax = jnp.max(l, axis=0, keepdims=True)
        rsum = jnp.sum(jnp.exp2(l - rmax), axis=1, keepdims=True)
        csum = jnp.sum(jnp.exp2(l - cmax), axis=0, keepdims=True)
        rlse = rmax + jnp.log(rsum) * LOG2E
        rowl[o, pl.ds(p, 1), :] = jnp.broadcast_to(rlse, (2 * R, R)).T[:1, :]
        coll[p, :, cols] = cmax + jnp.log(csum) * LOG2E

    def tiles(b, o, fresh):
        def step(i, carry):
            cc = lax.rem(c + i // 2, 2)
            p = cc * N + b * 2 + i % 2
            if fresh:

                @pl.when(i >= 2)
                def _():
                    for j in range(2):
                        for h in range(2):
                            itake(2 * p + j, h)

            tile(p, o)
            return carry

        lax.fori_loop(0, N, step, 0)

    tiles(yb, yo, True)
    k = islot(c, 1 - yb, x)
    itake(k, 1)
    igo(k, 1, sib)
    for h in (1, 0):
        for d in (1, 3, 2):
            k = islot(c, 1 - yb, turn(x, d))
            itake(k, h)
            igo(k, h, sib)
    for d in range(N):
        t = tslot(1 - yo, turn(z, d))
        ttake(t, 1)
        if d:
            ttake(t, 0)
    tiles(yb, 1 - yo, False)
    tiles(1 - yb, yo, True)
    tiles(1 - yb, 1 - yo, False)

    me = 2 * yb + c
    rowp[me] = lse2([rowl[0], rowl[1]])
    for dev in (by_i, by_is, sib):
        go(rowp.at[me], rowp.at[me], rp_r.at[me], dev)
    colp[yo] = lse2([coll[p] for p in range(PAIRS)])
    go(colp.at[yo], colp.at[yo], cp_r.at[yo], by_t)
    for v in (2 * yb + 1 - c, 2 - 2 * yb + c, 3 - 2 * yb - c):
        take(rowp.at[v], rp_r.at[v])
    rowx[x] = lse2([rowp[v] for v in range(N)])
    for d in range(1, N):
        go(rowx.at[x], rowx.at[x], rx_r.at[x], at_x(turn(x, d)))
    take(colp.at[1 - yo], cp_r.at[1 - yo])
    colz[z] = lse2([colp[0], colp[1]])
    for d in range(1, N):
        go(colz.at[z], colz.at[z], cz_r.at[z], at_z(turn(z, d)))
    for d in range(1, N):
        v = turn(x, d)
        take(rowx.at[v], rx_r.at[v])
    rowl[0] = lse2([rowx[v] for v in range(N)])
    for d in range(1, N):
        v = turn(z, d)
        take(colz.at[v], cz_r.at[v])
    coll[0] = lse2([colz[v] for v in range(N)])

    lane = lax.broadcasted_iota(jnp.int32, (8, R), 1)
    eye = lax.broadcasted_iota(jnp.int32, (R, R), 0) == lax.broadcasted_iota(jnp.int32, (R, R), 1)
    sums[0, c] = jnp.zeros((8, R), jnp.float32)

    def delta_step(p, total):
        l = logit[pair(p), :]
        lse = rowl[0, pl.ds(p, 1), :]
        rcol = jnp.broadcast_to(lse, (R, 2 * R)).T[:, :1]
        d = jnp.exp2(l - rcol) + jnp.exp2(l - coll[0])
        total = total + jnp.sum(d * l, axis=0, keepdims=True)
        delta[pair(p), :] = d.astype(jnp.bfloat16)
        for b in range(2):
            k = 2 * p + b
            irow = k % N * 2 + k // (2 * N)
            icol = (yo * 2 + k // N % 2) * N + z
            trow, tcol = icol % (2 * N), irow * 2 + icol // (2 * N)
            ty = tcol // N

            @pl.when(jnp.logical_and(trow == row, jnp.logical_or(ty == y, ty == yt)))
            def _():
                cols = block(tslot(ty // 2, tcol % N))
                sub = logit[block(k), cols]
                one = eye.astype(jnp.float32)
                rc = jnp.broadcast_to(lse[:, b * R : (b + 1) * R], (R, R)).T[:, :1]
                cc = coll[0, :, cols]
                fixed = (jnp.exp2(sub - rc) - one) + (jnp.exp2(sub - cc) - one)
                delta[block(k), cols] = fixed.astype(jnp.bfloat16)
                lossp = jnp.sum(jnp.where(eye, rc + cc - 2.0 * sub, 0.0), axis=0, keepdims=True)
                lossp = jnp.sum(lossp, axis=1, keepdims=True)
                diag = jnp.sum(jnp.where(eye, -2.0 * sub, 0.0), axis=0, keepdims=True)
                diag = jnp.sum(diag, axis=1, keepdims=True)
                sums[0, c] = sums[0, c] + jnp.where(lane == 0, lossp, jnp.where(lane == 1, diag, 0.0))

        return total

    total = lax.fori_loop(0, PAIRS, delta_step, jnp.zeros((1, TEXTS), jnp.float32))
    total = jnp.sum(total, axis=1, keepdims=True)
    sums[0, c] = sums[0, c] + jnp.where(lane == 1, total, 0.0)

    def sum_go(level, at, devs):
        for dev in devs:
            go(sums.at[level, at], sums.at[level, at], su_r.at[level, at], dev)

    def sum_take(level, at):
        take(sums.at[level, at], su_r.at[level, at])

    sum_go(0, c, [sib])

    ring_me, pair_me = (x, z), (yb, yo)
    ring_at, partner = (at_x, at_z), (by_i, by_t)
    stages = (stage_i, stage_t)

    def h0_copy(m, g, b, v):
        return send(
            stages[m].at[half(g, 0), :], a0.at[m, ring_me[m], b], pa0_s.at[m, g],
            pa0_r.at[m, ring_me[m], b], ring_at[m](v),
        )

    def h1_copy(m, g, v):
        return send(stages[m].at[half(g, 1), :], a1.at[m, v], pa1_s.at[m, g], pa1_r.at[m, v], partner[m])

    def emit(m, j, part):
        stages[m][pair(j), :] = part.astype(jnp.bfloat16)
        b = j // 2
        for i in range(2):
            g = 2 * j + i
            v = g % N

            @pl.when(v != ring_me[m])
            def _():
                h0_copy(m, g, b, v).start()

            @pl.when(v == ring_me[m])
            def _():
                own0[m, b] = part[i * R : i * R + H, :]

            @pl.when(b != pair_me[m])
            def _():
                h1_copy(m, g, v).start()

            @pl.when(b == pair_me[m])
            def _():
                own1[m, v] = part[i * R + H : (i + 1) * R, :]

    def sib_copy(j):
        return send(stage_s.at[pair(j), :], stage_c.at[pair(j), :], qc_s.at[j], qc_r.at[j], sib)

    def order(m, i):
        return lax.rem(pair_me[m] + 1 + i // 2, 2) * 2 + lax.rem(ring_me[m] // 2 + 1 + i, 2)

    def grad_step(i, carry):
        j = order(0, i)
        part = jnp.dot(delta[pair((1 - c) * N + j), :], txt[...], preferred_element_type=jnp.float32)
        stage_s[pair(j), :] = part.astype(jnp.bfloat16)
        sib_copy(j).start()
        q = order(1, i)
        emit(
            1, q,
            lax.dot_general(
                delta[:, pair(q)], img[...], (((0,), (0,)), ((), ())), preferred_element_type=jnp.float32
            ),
        )
        part = jnp.dot(delta[pair(c * N + j), :], txt[...], preferred_element_type=jnp.float32)
        sib_copy(j).wait_recv()
        emit(0, j, part + stage_c[pair(j), :].astype(jnp.float32))
        return carry

    lax.fori_loop(0, N, grad_step, 0)
    sum_take(0, 1 - c)
    sums[1, x] = sums[0, 0] + sums[0, 1]
    sum_go(1, x, [at_x(turn(x, d)) for d in range(1, N)])

    def h0_sum(m, b):
        acc = own0[m, b]
        for d in range(1, N):
            s = turn(ring_me[m], d)
            take(a0.at[m, s, b], pa0_r.at[m, s, b])
            acc = acc + a0[m, s, b].astype(jnp.float32)
        return acc

    def h1_sum(m, v):
        take(a1.at[m, v], pa1_r.at[m, v])
        return own1[m, v] + a1[m, v].astype(jnp.float32)

    for m in range(2):
        sb[m, 0] = h0_sum(m, 1 - pair_me[m]).astype(jnp.bfloat16)
        go(sb.at[m, 0], b0.at[m], pb0_r.at[m], partner[m])
    for d in range(1, N):
        for m in range(2):
            v = turn(ring_me[m], d)
            sb[m, d] = h1_sum(m, v).astype(jnp.bfloat16)
            go(sb.at[m, d], b1.at[m, ring_me[m]], pb1_r.at[m, ring_me[m]], ring_at[m](v))
    for d in range(1, N):
        sum_take(1, turn(x, d))
    sums[2, yb] = sums[1, 0] + sums[1, 1] + sums[1, 2] + sums[1, 3]
    sum_go(2, yb, [by_i])
    for m in range(2):
        own0[m, 0] = h0_sum(m, pair_me[m])
        own1[m, 0] = h1_sum(m, ring_me[m])
    sum_take(2, 1 - yb)
    sums[3, yo] = sums[2, 0] + sums[2, 1]
    sum_go(3, yo, [by_t])

    factor = scale * (1.0 / (2.0 * TEXTS * N * N))
    sources, results = (img_ref, txt_ref), (gi_ref, gt_ref)
    for m in range(2):
        take(b0.at[m], pb0_r.at[m])
        acc = own0[m, 0] + b0[m].astype(jnp.float32)
        results[m][:H, :] = project(sources[m][:H, :], factor * acc)
    sum_take(3, 1 - yo)
    sums[4, z] = sums[3, 0] + sums[3, 1]
    sum_go(4, z, [at_z(turn(z, d)) for d in range(1, N)])
    for m in range(2):
        acc = own1[m, 0]
        for d in range(1, N):
            s = turn(ring_me[m], d)
            take(b1.at[m, s], pb1_r.at[m, s])
            acc = acc + b1[m, s].astype(jnp.float32)
        results[m][H:, :] = project(sources[m][H:, :], factor * acc)
    for d in range(1, N):
        sum_take(4, turn(z, d))
    whole = (sums[4, 0] + sums[4, 1] + sums[4, 2] + sums[4, 3]) * (LN2 / (2.0 * TEXTS * N * N))
    top = lax.broadcasted_iota(jnp.int32, (8, R), 0) == 0
    loss_ref[0] = jnp.sum(jnp.where(jnp.logical_and(top, lane == 0), whole, 0.0))
    gs_ref[0] = jnp.sum(jnp.where(jnp.logical_and(top, lane == 1), whole, 0.0))

    for copy in started:
        copy.wait_send()

    def drain(g, carry):
        v, b = g % N, g // N
        for m in range(2):

            @pl.when(v != ring_me[m])
            def _():
                h0_copy(m, g, b, v).wait_send()

            @pl.when(b != pair_me[m])
            def _():
                h1_copy(m, g, v).wait_send()

        return carry

    lax.fori_loop(0, 2 * N, drain, 0)
    for j in range(N):
        sib_copy(j).wait_send()


def local(images, texts, log_scale):
    f32, bf16 = jnp.float32, jnp.bfloat16
    dma = pltpu.SemaphoreType.DMA
    vmem = pl.BlockSpec(memory_space=pltpu.VMEM)
    smem = pl.BlockSpec(memory_space=pltpu.SMEM)
    gi, gt, loss, gs = pl.pallas_call(
        kernel,
        out_shape=(
            jax.ShapeDtypeStruct((R, E), f32),
            jax.ShapeDtypeStruct((R, E), f32),
            jax.ShapeDtypeStruct((1,), f32),
            jax.ShapeDtypeStruct((1,), f32),
        ),
        in_specs=[vmem, vmem, smem],
        out_specs=(vmem, vmem, smem, smem),
        scratch_shapes=[
            pltpu.VMEM((IMAGES, E), bf16),
            pltpu.VMEM((TEXTS, E), bf16),
            pltpu.VMEM((IMAGES, TEXTS), f32),
            pltpu.VMEM((IMAGES, TEXTS), bf16),
            pltpu.VMEM((TEXTS, E), bf16),
            pltpu.VMEM((TEXTS, E), bf16),
            pltpu.VMEM((TEXTS, E), bf16),
            pltpu.VMEM((TEXTS, E), bf16),
            pltpu.VMEM((2, 2, H, E), f32),
            pltpu.VMEM((2, N, H, E), f32),
            pltpu.VMEM((2, N, 2, H, E), bf16),
            pltpu.VMEM((2, N, H, E), bf16),
            pltpu.VMEM((2, N, H, E), bf16),
            pltpu.VMEM((2, H, E), bf16),
            pltpu.VMEM((2, N, H, E), bf16),
            pltpu.VMEM((2, PAIRS, 2 * R), f32),
            pltpu.VMEM((N, PAIRS, 2 * R), f32),
            pltpu.VMEM((N, PAIRS, 2 * R), f32),
            pltpu.VMEM((PAIRS, 1, TEXTS), f32),
            pltpu.VMEM((2, 1, TEXTS), f32),
            pltpu.VMEM((N, 1, TEXTS), f32),
            pltpu.VMEM((5, N, 8, R), f32),
            dma((96,)),
            dma((N * N, 2)),
            dma((2 * N, 2)),
            dma((N,)), dma((N,)), dma((2,)), dma((N,)),
            dma((N,)), dma((N,)),
            dma((2, 2 * N)), dma((2, 2 * N)),
            dma((2, N, 2)), dma((2, N)),
            dma((2,)), dma((2, N)),
            dma((5, N)),
        ],
        compiler_params=pltpu.CompilerParams(
            collective_id=0, has_side_effects=True, vmem_limit_bytes=56 * 1024 * 1024
        ),
    )(images, texts, log_scale.reshape(1))
    return gi, gt, loss.reshape(()), gs.reshape(())


def solution(mesh):
    placed = (P(("row", "col"), None), P(("col", "row"), None), P())
    return jax.shard_map(
        local,
        mesh=mesh,
        in_specs=placed,
        out_specs=(P(("row", "col"), None), P(("col", "row"), None), P(), P()),
        check_vma=False,
    )
```

time: 351 us -> 78.2 us (0.22)
  blocking collectives: 164 us -> 0 us
  waiting for transfers between devices: 113 us -> 0 us
  Pallas kernels: 0 us -> 70.6 us
  other arithmetic: 30.9 us -> 0 us
  matrix products: 23.4 us -> 0 us
  between operations: 16.3 us -> 4.81 us
    psum x3 -> x0, blocking collectives: 113 us -> none  [the longest x1 64.3 us: local(): loss_sum, scale_sum = lax.psum((loss_part, scale_part), ('row', 'col'))]
    all_gather x2 -> x0, waiting for transfers between devices: 74.8 us -> none  [the longest x1 51.1 us: local(): image_block = lax.all_gather(image_low, 'col', axis=0, tiled=True)]
    pallas_call x0 -> x1, Pallas kernels: none -> 70.6 us  [local(): pl.pallas_call(kernel, out_shape=(jax.ShapeDtypeStruct((R, E), f32), jax....]
    pmax x2 -> x0, blocking collectives: 51 us -> none  [the longest x1 38.6 us: local(): row_peak = lax.pmax(jnp.max(logits, axis=1), 'col')]
    reduce_scatter x2 -> x0, waiting for transfers between devices: 38.3 us -> none  [the longest x1 38.3 us: local(): lax.psum_scatter(scale * jnp.dot(delta_low, text_block, preferred_element...]
    reduce_sum x7 -> x0, other arithmetic: 23.6 us -> none  [the longest x1 9.87 us: local(): scale_part = jnp.sum(delta * logits)]
    dot_general x3 -> x0, matrix products: 23.4 us -> none  [the longest x1 9.06 us: local(): jnp.dot(image_block, text_block.T, preferred_element_type=jnp.float32)]
    mul x2 -> x0, other arithmetic: 3.85 us -> none  [the longest x1 1.92 us: local(): text_inv * (text_grad - text_unit * jnp.sum(text_unit * text_grad, axis=1...]
  transfers between devices with their start and end apart: 4 -> 0, of which waited for: 3 -> 0; matrix products, arithmetic and copies ran while one was open for 4% -> 0% of each run, Pallas kernels for 0% -> 0%
where the time goes in v2:
time: 78.2 us; the launch traced here: 78 us
  Pallas kernels  70.6 us (90%)
  between operations  4.81 us (6%)
  local copies, waits for them, and re-layouts  2.57 us (3%)
    pallas_call x1, Pallas kernels, local(): pl.pallas_call(kernel, out_shape=(jax.ShapeDtypeStruct((R, E), f32), jax....  70.6 us
    unnamed x4, local copies, waits for them, and re-layouts  2.57 us

profile of v2, /device:TPU:0, one launch (start us, length us, event | category | flops | bytes accessed | tf_op | source)
XLA Modules:
  0.0 78.0 jit_solution(14054742017464886207)
XLA Ops:
  1.3 70.6 %shard_map.66 = (f32[128,768]{1,0:T(8,128)}, f32[128,768]{1,0:T(8,128)}, f32[1]{0:T(128)}, f32[1]{0:T(128)}) custom-call(bf16[128,768]{1,0:T(8,128)(2,1)} %img_ref.1, bf16[128,768]{1,0:T(8,128)(2,1)} %txt_ref.1, f32[1]{0:T(128)} %bitcast.3.scale_ref), custom_call_target="tpu_custom_call" | custom-call | tf_op jit(solution)/shard_map/pallas_call | solution.py:433
  71.9 0.0 copy-start
  71.9 1.8 %copy.12 = f32[128,768]{1,0:T(8,128)} copy(f32[128,768]{1,0:T(8,128)} %get-tuple-element.16) | data formatting | bytes 786432
  73.7 0.0 copy-done
  73.7 0.7 copy.13
Async XLA Ops:
  71.9 1.8 %copy-start = (f32[128,768]{1,0:T(8,128)S(1)}, f32[128,768]{1,0:T(8,128)}, u32[]{:S(2)}) copy-start(f32[128,768]{1,0:T(8,128)} %get-tuple-element.17) | copy-start | bytes 1179652

commit v3 on v2

--- a/solution.py
+++ b/solution.py
@@ -45,8 +45,8 @@
     img_ref, txt_ref, scale_ref, gi_ref, gt_ref, loss_ref, gs_ref,
     img, txt, logit, delta, stage_s, stage_c, stage_i, stage_t,
     own0, own1, a0, a1, sb, b0, b1,
-    rowl, rowp, rowx, coll, colp, colz, sums,
-    g_s, g_r, t_r, rp_r, rx_r, cp_r, cz_r, qc_s, qc_r, pa0_s, pa1_s, pa0_r, pa1_r, pb0_r, pb1_r, su_r,
+    rowl, rowp, rowx, coll, colz, sums,
+    g_s, g_r, t_r, rp_r, rx_r, cz_r, qc_s, qc_r, pa0_s, pa1_s, pa0_r, pa1_r, pb0_r, pb1_r, su_r,
 ):
     row, col = lax.axis_index("row"), lax.axis_index("col")
     x, c = row // 2, row % 2
@@ -57,8 +57,6 @@
     sib = (row + 1 - 2 * c, col)
     by_i = (row, yi * N + z)
     by_t = (row, yt * N + z)
-    by_is = (row + 1 - 2 * c, yi * N + z)
-
     def at_x(v):
         return (v * 2 + c, col)
 
@@ -67,6 +65,11 @@
 
     def turn(v, d):
         return lax.rem(v + d, N)
+
+    same_i = [at_x(turn(x, d)) for d in range(1, N)]
+    same_i += [(turn(x, d) * 2 + c, yi * N + z) for d in (1, 3, 2)] + [by_i]
+    same_t = [at_z(turn(z, d)) for d in range(1, N)]
+    same_t += [(row, yt * N + turn(z, d)) for d in (1, 3, 2)] + [by_t]
 
     def send(src, dst, ssem, rsem, dev):
         return pltpu.make_async_remote_copy(
@@ -84,9 +87,7 @@
         send(dst, dst, g_s.at[0], rsem, sib).wait_recv()
 
     barrier = pltpu.get_barrier_semaphore()
-    peers = [by_i, by_t, by_is, sib]
-    for d in range(1, N):
-        peers += [at_x(turn(x, d)), at_z(turn(z, d))]
+    peers = same_i + same_t + [sib]
     for dev in peers:
         pl.semaphore_signal(barrier, inc=1, device_id=dev, device_id_type=MESH)
 
@@ -164,38 +165,41 @@
     for d in (1, 3, 2):
         ttake(tslot(yo, turn(z, d)), 0)
 
-    def tile(p, o):
+    def tile(q, o):
+        rows = pl.ds(pl.multiple_of(q * N * R, N * R), N * R)
         cols = pl.ds(pl.multiple_of(o * N * R, N * R), N * R)
         l = scale2 * lax.dot_general(
-            img[pair(p), :], txt[cols, :], (((1,), (1,)), ((), ())), preferred_element_type=jnp.float32
+            img[rows, :], txt[cols, :], (((1,), (1,)), ((), ())), preferred_element_type=jnp.float32
         )
-        logit[pair(p), cols] = l
+        logit[rows, cols] = l
         rmax = jnp.max(l, axis=1, keepdims=True)
         cmax = jnp.max(l, axis=0, keepdims=True)
         rsum = jnp.sum(jnp.exp2(l - rmax), axis=1, keepdims=True)
         csum = jnp.sum(jnp.exp2(l - cmax), axis=0, keepdims=True)
         rlse = rmax + jnp.log(rsum) * LOG2E
-        rowl[o, pl.ds(p, 1), :] = jnp.broadcast_to(rlse, (2 * R, R)).T[:1, :]
-        coll[p, :, cols] = cmax + jnp.log(csum) * LOG2E
-
-    def tiles(b, o, fresh):
-        def step(i, carry):
-            cc = lax.rem(c + i // 2, 2)
-            p = cc * N + b * 2 + i % 2
-            if fresh:
-
-                @pl.when(i >= 2)
-                def _():
-                    for j in range(2):
-                        for h in range(2):
-                            itake(2 * p + j, h)
-
-            tile(p, o)
-            return carry
-
-        lax.fori_loop(0, N, step, 0)
-
-    tiles(yb, yo, True)
+        line = jnp.broadcast_to(rlse, (N * R, R)).T[:1, :]
+        for i in range(2):
+            rowl[o, pl.ds(2 * q + i, 1), :] = line[:, i * 2 * R : (i + 1) * 2 * R]
+        coll[q, :, cols] = cmax + jnp.log(csum) * LOG2E
+
+    def sib_blocks(b):
+        for v in range(N):
+            for h in range(2):
+                itake(islot(1 - c, b, v), h)
+
+    def tile_step(i, carry):
+        @pl.when(i == 1)
+        def _():
+            sib_blocks(yb)
+
+        @pl.when(i == 5)
+        def _():
+            sib_blocks(1 - yb)
+
+        tile(lax.rem(c + i, 2) * 2 + lax.rem(yb + i // 4, 2), lax.rem(yo + i // 2, 2))
+        return carry
+
+    lax.fori_loop(0, 2, tile_step, 0)
     k = islot(c, 1 - yb, x)
     itake(k, 1)
     igo(k, 1, sib)
@@ -209,72 +213,54 @@
         ttake(t, 1)
         if d:
             ttake(t, 0)
-    tiles(yb, 1 - yo, False)
-    tiles(1 - yb, yo, True)
-    tiles(1 - yb, 1 - yo, False)
-
-    me = 2 * yb + c
-    rowp[me] = lse2([rowl[0], rowl[1]])
-    for dev in (by_i, by_is, sib):
-        go(rowp.at[me], rowp.at[me], rp_r.at[me], dev)
-    colp[yo] = lse2([coll[p] for p in range(PAIRS)])
-    go(colp.at[yo], colp.at[yo], cp_r.at[yo], by_t)
-    for v in (2 * yb + 1 - c, 2 - 2 * yb + c, 3 - 2 * yb - c):
-        take(rowp.at[v], rp_r.at[v])
-    rowx[x] = lse2([rowp[v] for v in range(N)])
-    for d in range(1, N):
-        go(rowx.at[x], rowx.at[x], rx_r.at[x], at_x(turn(x, d)))
-    take(colp.at[1 - yo], cp_r.at[1 - yo])
-    colz[z] = lse2([colp[0], colp[1]])
-    for d in range(1, N):
-        go(colz.at[z], colz.at[z], cz_r.at[z], at_z(turn(z, d)))
-    for d in range(1, N):
-        v = turn(x, d)
-        take(rowx.at[v], rx_r.at[v])
-    rowl[0] = lse2([rowx[v] for v in range(N)])
-    for d in range(1, N):
-        v = turn(z, d)
-        take(colz.at[v], cz_r.at[v])
-    coll[0] = lse2([colz[v] for v in range(N)])
+    lax.fori_loop(2, 2 * N, tile_step, 0)
+
+    rowp[c] = lse2([rowl[0], rowl[1]])
+    go(rowp.at[c], rowp.at[c], rp_r.at[c], sib)
+    ime, tme = yb * N + x, yo * N + z
+    colz[tme] = lse2([coll[q] for q in range(N)])
+    for dev in same_t:
+        go(colz.at[tme], colz.at[tme], cz_r.at[tme], dev)
+    take(rowp.at[1 - c], rp_r.at[1 - c])
+    rowx[ime] = lse2([rowp[0], rowp[1]])
+    for dev in same_i:
+        go(rowx.at[ime], rowx.at[ime], rx_r.at[ime], dev)
+
+    def others(b, v):
+        return [b * N + turn(v, d) for d in range(1, N)] + [(1 - b) * N + turn(v, d) for d in range(N)]
+
+    for t in others(yo, z):
+        take(colz.at[t], cz_r.at[t])
+    coll[0] = lse2([colz[v] for v in range(2 * N)])
+    for t in others(yb, x):
+        take(rowx.at[t], rx_r.at[t])
+    rowl[0] = lse2([rowx[v] for v in range(2 * N)])
 
     lane = lax.broadcasted_iota(jnp.int32, (8, R), 1)
-    eye = lax.broadcasted_iota(jnp.int32, (R, R), 0) == lax.broadcasted_iota(jnp.int32, (R, R), 1)
-    sums[0, c] = jnp.zeros((8, R), jnp.float32)
-
-    def delta_step(p, total):
+
+    def meets(k):
+        irow = k % N * 2 + k // (2 * N)
+        icol = (yo * 2 + k // N % 2) * N + z
+        trow, tcol = icol % (2 * N), irow * 2 + icol // (2 * N)
+        ty = tcol // N
+        here = jnp.logical_and(trow == row, jnp.logical_or(ty == y, ty == yt))
+        return here, tslot(ty // 2, tcol % N)
+
+    def delta_part(p, total):
         l = logit[pair(p), :]
-        lse = rowl[0, pl.ds(p, 1), :]
-        rcol = jnp.broadcast_to(lse, (R, 2 * R)).T[:, :1]
-        d = jnp.exp2(l - rcol) + jnp.exp2(l - coll[0])
+        rcol = jnp.broadcast_to(rowl[0, pl.ds(p, 1), :], (R, 2 * R)).T[:, :1]
+        target = lax.broadcasted_iota(jnp.int32, (2 * R, 1), 0)
+        offs = []
+        for i in range(2):
+            here, slot = meets(2 * p + i)
+            offs.append(jnp.where(here, (slot - i) * R, -4 * TEXTS))
+        target = target + jnp.where(target < R, offs[0], offs[1])
+        twice = jnp.where(lax.broadcasted_iota(jnp.int32, (2 * R, TEXTS), 1) == target, 2.0, 0.0)
+        d = jnp.exp2(l - rcol) + jnp.exp2(l - coll[0]) - twice
         total = total + jnp.sum(d * l, axis=0, keepdims=True)
-        delta[pair(p), :] = d.astype(jnp.bfloat16)
-        for b in range(2):
-            k = 2 * p + b
-            irow = k % N * 2 + k // (2 * N)
-            icol = (yo * 2 + k // N % 2) * N + z
-            trow, tcol = icol % (2 * N), irow * 2 + icol // (2 * N)
-            ty = tcol // N
-
-            @pl.when(jnp.logical_and(trow == row, jnp.logical_or(ty == y, ty == yt)))
-            def _():
-                cols = block(tslot(ty // 2, tcol % N))
-                sub = logit[block(k), cols]
-                one = eye.astype(jnp.float32)
-                rc = jnp.broadcast_to(lse[:, b * R : (b + 1) * R], (R, R)).T[:, :1]
-                cc = coll[0, :, cols]
-                fixed = (jnp.exp2(sub - rc) - one) + (jnp.exp2(sub - cc) - one)
-                delta[block(k), cols] = fixed.astype(jnp.bfloat16)
-                lossp = jnp.sum(jnp.where(eye, rc + cc - 2.0 * sub, 0.0), axis=0, keepdims=True)
-                lossp = jnp.sum(lossp, axis=1, keepdims=True)
-                diag = jnp.sum(jnp.where(eye, -2.0 * sub, 0.0), axis=0, keepdims=True)
-                diag = jnp.sum(diag, axis=1, keepdims=True)
-                sums[0, c] = sums[0, c] + jnp.where(lane == 0, lossp, jnp.where(lane == 1, diag, 0.0))
-
-        return total
-
-    total = lax.fori_loop(0, PAIRS, delta_step, jnp.zeros((1, TEXTS), jnp.float32))
-    total = jnp.sum(total, axis=1, keepdims=True)
-    sums[0, c] = sums[0, c] + jnp.where(lane == 1, total, 0.0)
+        low = d.astype(jnp.bfloat16)
+        delta[pair(p), :] = low
+        return jnp.dot(low, txt[...], preferred_element_type=jnp.float32), total
 
     def sum_go(level, at, devs):
         for dev in devs:
@@ -282,8 +268,6 @@
 
     def sum_take(level, at):
         take(sums.at[level, at], su_r.at[level, at])
-
-    sum_go(0, c, [sib])
 
     ring_me, pair_me = (x, z), (yb, yo)
     ring_at, partner = (at_x, at_z), (by_i, by_t)
@@ -327,11 +311,22 @@
     def order(m, i):
         return lax.rem(pair_me[m] + 1 + i // 2, 2) * 2 + lax.rem(ring_me[m] // 2 + 1 + i, 2)
 
-    def grad_step(i, carry):
-        j = order(0, i)
-        part = jnp.dot(delta[pair((1 - c) * N + j), :], txt[...], preferred_element_type=jnp.float32)
-        stage_s[pair(j), :] = part.astype(jnp.bfloat16)
-        sib_copy(j).start()
+    def image_step(i, total):
+        for u in range(2):
+            j = order(0, 2 * i + u)
+            part, total = delta_part((1 - c) * N + j, total)
+            stage_s[pair(j), :] = part.astype(jnp.bfloat16)
+            sib_copy(j).start()
+        for u in range(2):
+            j = order(0, 2 * i + u)
+            part, total = delta_part(c * N + j, total)
+            sib_copy(j).wait_recv()
+            emit(0, j, part + stage_c[pair(j), :].astype(jnp.float32))
+        return total
+
+    total = lax.fori_loop(0, 2, image_step, jnp.zeros((1, TEXTS), jnp.float32))
+
+    def text_step(i, carry):
         q = order(1, i)
         emit(
             1, q,
@@ -339,15 +334,29 @@
                 delta[:, pair(q)], img[...], (((0,), (0,)), ((), ())), preferred_element_type=jnp.float32
             ),
         )
-        part = jnp.dot(delta[pair(c * N + j), :], txt[...], preferred_element_type=jnp.float32)
-        sib_copy(j).wait_recv()
-        emit(0, j, part + stage_c[pair(j), :].astype(jnp.float32))
         return carry
 
-    lax.fori_loop(0, N, grad_step, 0)
-    sum_take(0, 1 - c)
-    sums[1, x] = sums[0, 0] + sums[0, 1]
-    sum_go(1, x, [at_x(turn(x, d)) for d in range(1, N)])
+    lax.fori_loop(0, N, text_step, 0)
+
+    sums[0, c] = jnp.where(lane == 1, jnp.sum(total, axis=1, keepdims=True), jnp.zeros((8, R), jnp.float32))
+    eye = lax.broadcasted_iota(jnp.int32, (R, R), 0) == lax.broadcasted_iota(jnp.int32, (R, R), 1)
+
+    def loss_step(k, carry):
+        here, slot = meets(k)
+
+        @pl.when(here)
+        def _():
+            cols = block(slot)
+            both = rowl[0, pl.ds(k // 2, 1), :]
+            rl = jnp.where(k % 2 == 0, both[:, :R], both[:, R:])
+            pairs = jnp.sum(jnp.where(eye, logit[block(k), cols], 0.0), axis=0, keepdims=True)
+            part = jnp.sum(rl + coll[0, :, cols] - 2.0 * pairs, axis=1, keepdims=True)
+            sums[0, c] = sums[0, c] + jnp.where(lane == 0, part, 0.0)
+
+        return carry
+
+    lax.fori_loop(0, N * N, loss_step, 0)
+    sum_go(0, c, [sib])
 
     def h0_sum(m, b):
         acc = own0[m, b]
@@ -361,24 +370,28 @@
         take(a1.at[m, v], pa1_r.at[m, v])
         return own1[m, v] + a1[m, v].astype(jnp.float32)
 
-    for m in range(2):
+    def second(m):
         sb[m, 0] = h0_sum(m, 1 - pair_me[m]).astype(jnp.bfloat16)
         go(sb.at[m, 0], b0.at[m], pb0_r.at[m], partner[m])
-    for d in range(1, N):
-        for m in range(2):
+        for d in (2, 1, 3):
             v = turn(ring_me[m], d)
             sb[m, d] = h1_sum(m, v).astype(jnp.bfloat16)
             go(sb.at[m, d], b1.at[m, ring_me[m]], pb1_r.at[m, ring_me[m]], ring_at[m](v))
-    for d in range(1, N):
-        sum_take(1, turn(x, d))
-    sums[2, yb] = sums[1, 0] + sums[1, 1] + sums[1, 2] + sums[1, 3]
-    sum_go(2, yb, [by_i])
-    for m in range(2):
         own0[m, 0] = h0_sum(m, pair_me[m])
         own1[m, 0] = h1_sum(m, ring_me[m])
-    sum_take(2, 1 - yb)
-    sums[3, yo] = sums[2, 0] + sums[2, 1]
-    sum_go(3, yo, [by_t])
+
+    second(0)
+    sum_take(0, 1 - c)
+    sums[1, ime] = sums[0, 0] + sums[0, 1]
+    sum_go(1, ime, same_i)
+    second(1)
+    for t in others(yb, x):
+        sum_take(1, t)
+    acc = sums[1, 0]
+    for v in range(1, 2 * N):
+        acc = acc + sums[1, v]
+    sums[2, tme] = acc
+    sum_go(2, tme, same_t)
 
     factor = scale * (1.0 / (2.0 * TEXTS * N * N))
     sources, results = (img_ref, txt_ref), (gi_ref, gt_ref)
@@ -386,19 +399,18 @@
         take(b0.at[m], pb0_r.at[m])
         acc = own0[m, 0] + b0[m].astype(jnp.float32)
         results[m][:H, :] = project(sources[m][:H, :], factor * acc)
-    sum_take(3, 1 - yo)
-    sums[4, z] = sums[3, 0] + sums[3, 1]
-    sum_go(4, z, [at_z(turn(z, d)) for d in range(1, N)])
-    for m in range(2):
         acc = own1[m, 0]
         for d in range(1, N):
             s = turn(ring_me[m], d)
             take(b1.at[m, s], pb1_r.at[m, s])
             acc = acc + b1[m, s].astype(jnp.float32)
         results[m][H:, :] = project(sources[m][H:, :], factor * acc)
-    for d in range(1, N):
-        sum_take(4, turn(z, d))
-    whole = (sums[4, 0] + sums[4, 1] + sums[4, 2] + sums[4, 3]) * (LN2 / (2.0 * TEXTS * N * N))
+    for t in others(yo, z):
+        sum_take(2, t)
+    whole = sums[2, 0]
+    for v in range(1, 2 * N):
+        whole = whole + sums[2, v]
+    whole = whole * (LN2 / (2.0 * TEXTS * N * N))
     top = lax.broadcasted_iota(jnp.int32, (8, R), 0) == 0
     loss_ref[0] = jnp.sum(jnp.where(jnp.logical_and(top, lane == 0), whole, 0.0))
     gs_ref[0] = jnp.sum(jnp.where(jnp.logical_and(top, lane == 1), whole, 0.0))
@@ -457,21 +469,20 @@
             pltpu.VMEM((2, H, E), bf16),
             pltpu.VMEM((2, N, H, E), bf16),
             pltpu.VMEM((2, PAIRS, 2 * R), f32),
-            pltpu.VMEM((N, PAIRS, 2 * R), f32),
-            pltpu.VMEM((N, PAIRS, 2 * R), f32),
-            pltpu.VMEM((PAIRS, 1, TEXTS), f32),
-            pltpu.VMEM((2, 1, TEXTS), f32),
+            pltpu.VMEM((2, PAIRS, 2 * R), f32),
+            pltpu.VMEM((2 * N, PAIRS, 2 * R), f32),
             pltpu.VMEM((N, 1, TEXTS), f32),
-            pltpu.VMEM((5, N, 8, R), f32),
+            pltpu.VMEM((2 * N, 1, TEXTS), f32),
+            pltpu.VMEM((3, 2 * N, 8, R), f32),
             dma((96,)),
             dma((N * N, 2)),
             dma((2 * N, 2)),
-            dma((N,)), dma((N,)), dma((2,)), dma((N,)),
+            dma((2,)), dma((2 * N,)), dma((2 * N,)),
             dma((N,)), dma((N,)),
             dma((2, 2 * N)), dma((2, 2 * N)),
             dma((2, N, 2)), dma((2, N)),
             dma((2,)), dma((2, N)),
-            dma((5, N)),
+            dma((3, 2 * N)),
         ],
         compiler_params=pltpu.CompilerParams(
             collective_id=0, has_side_effects=True, vmem_limit_bytes=56 * 1024 * 1024

time: 78.2 us -> 72.8 us (0.931)
  Pallas kernels: 70.6 us -> 65.2 us
    pallas_call x1, Pallas kernels: 70.6 us -> 65.2 us  [local(): pl.pallas_call(kernel, out_shape=(jax.ShapeDtypeStruct((R, E), f32), jax....]
where the time goes in v3:
time: 72.8 us; the launch traced here: 72.6 us
  Pallas kernels  65.2 us (90%)
  between operations  4.81 us (7%)
  local copies, waits for them, and re-layouts  2.57 us (4%)
    pallas_call x1, Pallas kernels, local(): pl.pallas_call(kernel, out_shape=(jax.ShapeDtypeStruct((R, E), f32), jax....  65.2 us
    unnamed x4, local copies, waits for them, and re-layouts  2.57 us

profile of v3, /device:TPU:0, one launch (start us, length us, event | category | flops | bytes accessed | tf_op | source)
XLA Modules:
  0.0 72.6 jit_solution(16077652539076509256)
XLA Ops:
  1.3 65.2 %shard_map.66 = (f32[128,768]{1,0:T(8,128)}, f32[128,768]{1,0:T(8,128)}, f32[1]{0:T(128)}, f32[1]{0:T(128)}) custom-call(bf16[128,768]{1,0:T(8,128)(2,1)} %img_ref.1, bf16[128,768]{1,0:T(8,128)(2,1)} %txt_ref.1, f32[1]{0:T(128)} %bitcast.3.scale_ref), custom_call_target="tpu_custom_call" | custom-call | tf_op jit(solution)/shard_map/pallas_call | solution.py:445
  66.5 0.0 copy-start
  66.5 1.8 %copy.12 = f32[128,768]{1,0:T(8,128)} copy(f32[128,768]{1,0:T(8,128)} %get-tuple-element.16) | data formatting | bytes 786432
  68.3 0.0 copy-done
  68.3 0.7 %copy.13 = f32[128,768]{1,0:T(8,128)} copy(f32[128,768]{1,0:T(8,128)S(1)} %copy-done) | data formatting | bytes 786432
Async XLA Ops:
  66.5 1.8 %copy-start = (f32[128,768]{1,0:T(8,128)S(1)}, f32[128,768]{1,0:T(8,128)}, u32[]{:S(2)}) copy-start(f32[128,768]{1,0:T(8,128)} %get-tuple-element.17) | copy-start | bytes 1179652

commit v4 on v3

--- a/solution.py
+++ b/solution.py
@@ -44,7 +44,7 @@
 def kernel(
     img_ref, txt_ref, scale_ref, gi_ref, gt_ref, loss_ref, gs_ref,
     img, txt, logit, delta, stage_s, stage_c, stage_i, stage_t,
-    own0, own1, a0, a1, sb, b0, b1,
+    own0, own1, fin, a0, a1, sb, b0, b1,
     rowl, rowp, rowx, coll, colz, sums,
     g_s, g_r, t_r, rp_r, rx_r, cz_r, qc_s, qc_r, pa0_s, pa1_s, pa0_r, pa1_r, pb0_r, pb1_r, su_r,
 ):
@@ -87,7 +87,7 @@
         send(dst, dst, g_s.at[0], rsem, sib).wait_recv()
 
     barrier = pltpu.get_barrier_semaphore()
-    peers = same_i + same_t + [sib]
+    peers = same_i[: N - 1] + same_t[: N - 1] + [by_i, by_t, sib]
     for dev in peers:
         pl.semaphore_signal(barrier, inc=1, device_id=dev, device_id_type=MESH)
 
@@ -282,61 +282,66 @@
     def h1_copy(m, g, v):
         return send(stages[m].at[half(g, 1), :], a1.at[m, v], pa1_s.at[m, g], pa1_r.at[m, v], partner[m])
 
-    def emit(m, j, part):
-        stages[m][pair(j), :] = part.astype(jnp.bfloat16)
-        b = j // 2
-        for i in range(2):
-            g = 2 * j + i
-            v = g % N
-
-            @pl.when(v != ring_me[m])
-            def _():
-                h0_copy(m, g, b, v).start()
-
-            @pl.when(v == ring_me[m])
-            def _():
-                own0[m, b] = part[i * R : i * R + H, :]
-
-            @pl.when(b != pair_me[m])
-            def _():
-                h1_copy(m, g, v).start()
-
-            @pl.when(b == pair_me[m])
-            def _():
-                own1[m, v] = part[i * R + H : (i + 1) * R, :]
+    def spot(m, i):
+        b = pair_me[m] if i // 2 else 1 - pair_me[m]
+        near = ring_me[m] // 2
+        return b, near if i % 2 else 1 - near
+
+    def order(m, i):
+        b, half_ring = spot(m, i)
+        return b * 2 + half_ring
+
+    def twin(m):
+        return ring_me[m] + 1 - ring_me[m] % 2 * 2
+
+    def emit(m, i, part):
+        b, half_ring = spot(m, i)
+        stages[m][pair(order(m, i)), :] = part.astype(jnp.bfloat16)
+        for t in range(2):
+            v = 2 * half_ring + t
+            if i % 2:
+                own0[m, i // 2, t] = part[t * R : t * R + H, :]
+            else:
+                h0_copy(m, b * N + v, b, v).start()
+            if i // 2:
+                own1[m, v] = part[t * R + H : (t + 1) * R, :]
+            else:
+                h1_copy(m, b * N + v, v).start()
+        if i % 2:
+            h0_copy(m, b * N + twin(m), b, twin(m)).start()
 
     def sib_copy(j):
         return send(stage_s.at[pair(j), :], stage_c.at[pair(j), :], qc_s.at[j], qc_r.at[j], sib)
 
-    def order(m, i):
-        return lax.rem(pair_me[m] + 1 + i // 2, 2) * 2 + lax.rem(ring_me[m] // 2 + 1 + i, 2)
-
-    def image_step(i, total):
-        for u in range(2):
-            j = order(0, 2 * i + u)
+    def sib_step(i, total):
+        js = [lax.rem(1 - yb + i, 2) * 2 + v for v in (1 - x // 2, x // 2)]
+        for j in js:
             part, total = delta_part((1 - c) * N + j, total)
             stage_s[pair(j), :] = part.astype(jnp.bfloat16)
+        for j in js:
             sib_copy(j).start()
+        return total
+
+    total = lax.fori_loop(0, 2, sib_step, jnp.zeros((1, TEXTS), jnp.float32))
+    for i in (0, 2):
+        parts = []
         for u in range(2):
-            j = order(0, 2 * i + u)
-            part, total = delta_part(c * N + j, total)
+            part, total = delta_part(c * N + order(0, i + u), total)
+            parts.append(part)
+        for u in range(2):
+            j = order(0, i + u)
             sib_copy(j).wait_recv()
-            emit(0, j, part + stage_c[pair(j), :].astype(jnp.float32))
-        return total
-
-    total = lax.fori_loop(0, 2, image_step, jnp.zeros((1, TEXTS), jnp.float32))
-
-    def text_step(i, carry):
-        q = order(1, i)
-        emit(
-            1, q,
-            lax.dot_general(
-                delta[:, pair(q)], img[...], (((0,), (0,)), ((), ())), preferred_element_type=jnp.float32
-            ),
+            emit(0, i + u, parts[u] + stage_c[pair(j), :].astype(jnp.float32))
+
+    def text_part(i):
+        return lax.dot_general(
+            delta[:, pair(order(1, i))], img[...], (((0,), (0,)), ((), ())), preferred_element_type=jnp.float32
         )
-        return carry
-
-    lax.fori_loop(0, N, text_step, 0)
+
+    for i in (0, 2):
+        parts = [text_part(i), text_part(i + 1)]
+        for u in range(2):
+            emit(1, i + u, parts[u])
 
     sums[0, c] = jnp.where(lane == 1, jnp.sum(total, axis=1, keepdims=True), jnp.zeros((8, R), jnp.float32))
     eye = lax.broadcasted_iota(jnp.int32, (R, R), 0) == lax.broadcasted_iota(jnp.int32, (R, R), 1)
@@ -358,8 +363,9 @@
     lax.fori_loop(0, N * N, loss_step, 0)
     sum_go(0, c, [sib])
 
-    def h0_sum(m, b):
-        acc = own0[m, b]
+    def h0_sum(m, i):
+        b = pair_me[m] if i else 1 - pair_me[m]
+        acc = own0[m, i, ring_me[m] % 2]
         for d in range(1, N):
             s = turn(ring_me[m], d)
             take(a0.at[m, s, b], pa0_r.at[m, s, b])
@@ -370,21 +376,29 @@
         take(a1.at[m, v], pa1_r.at[m, v])
         return own1[m, v] + a1[m, v].astype(jnp.float32)
 
-    def second(m):
-        sb[m, 0] = h0_sum(m, 1 - pair_me[m]).astype(jnp.bfloat16)
-        go(sb.at[m, 0], b0.at[m], pb0_r.at[m], partner[m])
-        for d in (2, 1, 3):
-            v = turn(ring_me[m], d)
-            sb[m, d] = h1_sum(m, v).astype(jnp.bfloat16)
-            go(sb.at[m, d], b1.at[m, ring_me[m]], pb1_r.at[m, ring_me[m]], ring_at[m](v))
-        own0[m, 0] = h0_sum(m, pair_me[m])
-        own1[m, 0] = h1_sum(m, ring_me[m])
-
-    second(0)
+    def second0(m):
+        sb[m, N] = h0_sum(m, 0).astype(jnp.bfloat16)
+        go(sb.at[m, N], b0.at[m], pb0_r.at[m], partner[m])
+
+    def second1(m, v):
+        sb[m, v] = h1_sum(m, v).astype(jnp.bfloat16)
+        go(sb.at[m, v], b1.at[m, ring_me[m]], pb1_r.at[m, ring_me[m]], ring_at[m](v))
+
+    def far_blocks(m):
+        v = 2 - ring_me[m] // 2 * 2
+        return v, v + 1
+
+    for v in far_blocks(0):
+        second1(0, v)
+    second0(0)
     sum_take(0, 1 - c)
     sums[1, ime] = sums[0, 0] + sums[0, 1]
     sum_go(1, ime, same_i)
-    second(1)
+    for v in far_blocks(1):
+        second1(1, v)
+    second1(0, twin(0))
+    second0(1)
+    second1(1, twin(1))
     for t in others(yb, x):
         sum_take(1, t)
     acc = sums[1, 0]
@@ -392,14 +406,17 @@
         acc = acc + sums[1, v]
     sums[2, tme] = acc
     sum_go(2, tme, same_t)
+    for m in range(2):
+        fin[m, 0] = h0_sum(m, 1)
+        fin[m, 1] = h1_sum(m, ring_me[m])
 
     factor = scale * (1.0 / (2.0 * TEXTS * N * N))
     sources, results = (img_ref, txt_ref), (gi_ref, gt_ref)
     for m in range(2):
         take(b0.at[m], pb0_r.at[m])
-        acc = own0[m, 0] + b0[m].astype(jnp.float32)
+        acc = fin[m, 0] + b0[m].astype(jnp.float32)
         results[m][:H, :] = project(sources[m][:H, :], factor * acc)
-        acc = own1[m, 0]
+        acc = fin[m, 1]
         for d in range(1, N):
             s = turn(ring_me[m], d)
             take(b1.at[m, s], pb1_r.at[m, s])
@@ -418,21 +435,13 @@
     for copy in started:
         copy.wait_send()
 
-    def drain(g, carry):
-        v, b = g % N, g // N
-        for m in range(2):
-
-            @pl.when(v != ring_me[m])
-            def _():
-                h0_copy(m, g, b, v).wait_send()
-
-            @pl.when(b != pair_me[m])
-            def _():
-                h1_copy(m, g, v).wait_send()
-
-        return carry
-
-    lax.fori_loop(0, 2 * N, drain, 0)
+    for m in range(2):
+        for b in range(2):
+            for d in range(1, N):
+                v = turn(ring_me[m], d)
+                h0_copy(m, b * N + v, b, v).wait_send()
+        for v in range(N):
+            h1_copy(m, (1 - pair_me[m]) * N + v, v).wait_send()
     for j in range(N):
         sib_copy(j).wait_send()
 
@@ -461,11 +470,12 @@
             pltpu.VMEM((TEXTS, E), bf16),
             pltpu.VMEM((TEXTS, E), bf16),
             pltpu.VMEM((TEXTS, E), bf16),
+            pltpu.VMEM((2, 2, 2, H, E), f32),
+            pltpu.VMEM((2, N, H, E), f32),
             pltpu.VMEM((2, 2, H, E), f32),
-            pltpu.VMEM((2, N, H, E), f32),
             pltpu.VMEM((2, N, 2, H, E), bf16),
             pltpu.VMEM((2, N, H, E), bf16),
-            pltpu.VMEM((2, N, H, E), bf16),
+            pltpu.VMEM((2, N + 1, H, E), bf16),
             pltpu.VMEM((2, H, E), bf16),
             pltpu.VMEM((2, N, H, E), bf16),
             pltpu.VMEM((2, PAIRS, 2 * R), f32),

time: 72.8 us -> 70.8 us (0.973)
  Pallas kernels: 65.2 us -> 62.6 us
    pallas_call x1, Pallas kernels: 65.2 us -> 62.6 us  [local(): pl.pallas_call(kernel, out_shape=(jax.ShapeDtypeStruct((R, E), f32), jax....]
where the time goes in v4:
time: 70.8 us; the launch traced here: 70 us
  Pallas kernels  62.6 us (88%)
  between operations  4.81 us (7%)
  local copies, waits for them, and re-layouts  2.57 us (4%)
    pallas_call x1, Pallas kernels, local(): pl.pallas_call(kernel, out_shape=(jax.ShapeDtypeStruct((R, E), f32), jax....  62.6 us
    unnamed x4, local copies, waits for them, and re-layouts  2.57 us

profile of v4, /device:TPU:0, one launch (start us, length us, event | category | flops | bytes accessed | tf_op | source)
XLA Modules:
  0.0 70.0 jit_solution(17186177251691087156)
XLA Ops:
  1.3 62.6 %shard_map.66 = (f32[128,768]{1,0:T(8,128)}, f32[128,768]{1,0:T(8,128)}, f32[1]{0:T(128)}, f32[1]{0:T(128)}) custom-call(bf16[128,768]{1,0:T(8,128)(2,1)} %img_ref.1, bf16[128,768]{1,0:T(8,128)(2,1)} %txt_ref.1, f32[1]{0:T(128)} %bitcast.3.scale_ref), custom_call_target="tpu_custom_call" | custom-call | tf_op jit(solution)/shard_map/pallas_call | solution.py:454
  63.9 0.0 copy-start
  63.9 1.8 %copy.12 = f32[128,768]{1,0:T(8,128)} copy(f32[128,768]{1,0:T(8,128)} %get-tuple-element.16) | data formatting | bytes 786432
  65.7 0.0 copy-done
  65.7 0.7 %copy.13 = f32[128,768]{1,0:T(8,128)} copy(f32[128,768]{1,0:T(8,128)S(1)} %copy-done) | data formatting | bytes 786432
Async XLA Ops:
  63.9 1.8 %copy-start = (f32[128,768]{1,0:T(8,128)S(1)}, f32[128,768]{1,0:T(8,128)}, u32[]{:S(2)}) copy-start(f32[128,768]{1,0:T(8,128)} %get-tuple-element.17) | copy-start | bytes 1179652

commit v5 on v4

--- a/solution.py
+++ b/solution.py
@@ -66,6 +66,8 @@
     def turn(v, d):
         return lax.rem(v + d, N)
 
+    x_up, x_down, z_up, z_down = turn(x, 1), turn(x, 3), turn(z, 1), turn(z, 3)
+
     same_i = [at_x(turn(x, d)) for d in range(1, N)]
     same_i += [(turn(x, d) * 2 + c, yi * N + z) for d in (1, 3, 2)] + [by_i]
     same_t = [at_z(turn(z, d)) for d in range(1, N)]
@@ -87,7 +89,7 @@
         send(dst, dst, g_s.at[0], rsem, sib).wait_recv()
 
     barrier = pltpu.get_barrier_semaphore()
-    peers = same_i[: N - 1] + same_t[: N - 1] + [by_i, by_t, sib]
+    peers = [at_x(x_up), at_x(x_down), at_z(z_up), at_z(z_down), by_i, by_t, sib]
     for dev in peers:
         pl.semaphore_signal(barrier, inc=1, device_id=dev, device_id_type=MESH)
 
@@ -134,44 +136,53 @@
     igo(imine, 0, by_i)
     tgo(tmine, 0, by_t)
     for h in (1, 0):
-        for d in range(1, N):
-            igo(imine, h, at_x(turn(x, d)))
-            tgo(tmine, h, at_z(turn(z, d)))
+        for v, w in ((x_up, z_up), (x_down, z_down)):
+            igo(imine, h, at_x(v))
+            tgo(tmine, h, at_z(w))
     igo(imine, 1, by_i)
     tgo(tmine, 1, by_t)
     for h in range(2):
         igo(imine, h, sib)
-    k = islot(c, 1 - yb, x)
-    itake(k, 0)
-    for d in range(1, N):
-        igo(k, 0, at_x(turn(x, d)))
-    t = tslot(1 - yo, z)
-    ttake(t, 0)
-    for d in range(1, N):
-        tgo(t, 0, at_z(turn(z, d)))
-    igo(k, 0, sib)
-    for d in (1, 3, 2):
-        k = islot(c, yb, turn(x, d))
-        itake(k, 1)
-        igo(k, 1, by_i)
-        igo(k, 1, sib)
-        t = tslot(yo, turn(z, d))
-        ttake(t, 1)
-        tgo(t, 1, by_t)
-    for d in (1, 3, 2):
-        k = islot(c, yb, turn(x, d))
-        itake(k, 0)
-        igo(k, 0, sib)
-    for d in (1, 3, 2):
-        ttake(tslot(yo, turn(z, d)), 0)
-
-    def tile(q, o):
+
+    def ipass(b, v, h, devs):
+        k = islot(c, b, v)
+        itake(k, h)
+        for dev in devs + [sib]:
+            igo(k, h, dev)
+
+    def tpass(o, v, h, devs):
+        k = tslot(o, v)
+        ttake(k, h)
+        for dev in devs:
+            tgo(k, h, dev)
+
+    ipass(yb, x_down, 1, [at_x(x_up), by_i])
+    tpass(yo, z_down, 1, [at_z(z_up), by_t])
+    ipass(1 - yb, x, 0, [at_x(x_up), at_x(x_down)])
+    tpass(1 - yo, z, 0, [at_z(z_up), at_z(z_down)])
+    ipass(yb, x_up, 1, [by_i])
+    tpass(yo, z_up, 1, [by_t])
+    ipass(yb, x_up, 0, [at_x(x_down)])
+    tpass(yo, z_up, 0, [at_z(z_down)])
+    ipass(yb, x_down, 0, [])
+    tpass(yo, z_down, 0, [])
+    ipass(yb, turn(x, 2), 1, [by_i])
+    tpass(yo, turn(z, 2), 1, [by_t])
+    ipass(1 - yb, turn(x, 3 - 2 * c), 0, [at_x(turn(x, 1 + 2 * c))])
+    tpass(1 - yo, turn(z, 3 - 2 * c), 0, [at_z(turn(z, 1 + 2 * c))])
+    ipass(yb, turn(x, 2), 0, [])
+    tpass(yo, turn(z, 2), 0, [])
+
+    def tile_logits(q, o):
         rows = pl.ds(pl.multiple_of(q * N * R, N * R), N * R)
         cols = pl.ds(pl.multiple_of(o * N * R, N * R), N * R)
         l = scale2 * lax.dot_general(
             img[rows, :], txt[cols, :], (((1,), (1,)), ((), ())), preferred_element_type=jnp.float32
         )
         logit[rows, cols] = l
+        return q, o, cols, l
+
+    def tile_lse(q, o, cols, l):
         rmax = jnp.max(l, axis=1, keepdims=True)
         cmax = jnp.max(l, axis=0, keepdims=True)
         rsum = jnp.sum(jnp.exp2(l - rmax), axis=1, keepdims=True)
@@ -187,33 +198,33 @@
             for h in range(2):
                 itake(islot(1 - c, b, v), h)
 
+    def spot_of(i):
+        return lax.rem(c + i, 2) * 2 + lax.rem(yb + i // 4, 2), lax.rem(yo + i // 2, 2)
+
     def tile_step(i, carry):
-        @pl.when(i == 1)
-        def _():
-            sib_blocks(yb)
-
-        @pl.when(i == 5)
+        @pl.when(i == 2)
         def _():
             sib_blocks(1 - yb)
 
-        tile(lax.rem(c + i, 2) * 2 + lax.rem(yb + i // 4, 2), lax.rem(yo + i // 2, 2))
+        made = [tile_logits(*spot_of(2 * i + u)) for u in range(2)]
+        for one in made:
+            tile_lse(*one)
         return carry
 
-    lax.fori_loop(0, 2, tile_step, 0)
-    k = islot(c, 1 - yb, x)
-    itake(k, 1)
-    igo(k, 1, sib)
-    for h in (1, 0):
-        for d in (1, 3, 2):
-            k = islot(c, 1 - yb, turn(x, d))
-            itake(k, h)
-            igo(k, h, sib)
-    for d in range(N):
-        t = tslot(1 - yo, turn(z, d))
-        ttake(t, 1)
-        if d:
-            ttake(t, 0)
-    lax.fori_loop(2, 2 * N, tile_step, 0)
+    tile_lse(*tile_logits(*spot_of(0)))
+    sib_blocks(yb)
+    tile_lse(*tile_logits(*spot_of(1)))
+    ipass(1 - yb, x, 1, [])
+    for v in (x_down, x_up):
+        ipass(1 - yb, v, 1, [])
+    ipass(1 - yb, turn(x, 1 + 2 * c), 0, [])
+    ipass(1 - yb, turn(x, 2), 1, [])
+    ipass(1 - yb, turn(x, 2), 0, [])
+    for v in (z, z_down, z_up, turn(z, 2)):
+        tpass(1 - yo, v, 1, [])
+    tpass(1 - yo, turn(z, 1 + 2 * c), 0, [])
+    tpass(1 - yo, turn(z, 2), 0, [])
+    lax.fori_loop(1, N, tile_step, 0)
 
     rowp[c] = lse2([rowl[0], rowl[1]])
     go(rowp.at[c], rowp.at[c], rp_r.at[c], sib)
@@ -260,7 +271,10 @@
         total = total + jnp.sum(d * l, axis=0, keepdims=True)
         low = d.astype(jnp.bfloat16)
         delta[pair(p), :] = low
-        return jnp.dot(low, txt[...], preferred_element_type=jnp.float32), total
+        return low, total
+
+    def image_part(low):
+        return jnp.dot(low, txt[...], preferred_element_type=jnp.float32)
 
     def sum_go(level, at, devs):
         for dev in devs:
@@ -313,36 +327,46 @@
     def sib_copy(j):
         return send(stage_s.at[pair(j), :], stage_c.at[pair(j), :], qc_s.at[j], qc_r.at[j], sib)
 
-    def sib_step(i, total):
-        js = [lax.rem(1 - yb + i, 2) * 2 + v for v in (1 - x // 2, x // 2)]
-        for j in js:
-            part, total = delta_part((1 - c) * N + j, total)
-            stage_s[pair(j), :] = part.astype(jnp.bfloat16)
-        for j in js:
-            sib_copy(j).start()
+    def sib_part(i, total):
+        j = order(0, i)
+        low, total = delta_part((1 - c) * N + j, total)
+        stage_s[pair(j), :] = image_part(low).astype(jnp.bfloat16)
         return total
 
-    total = lax.fori_loop(0, 2, sib_step, jnp.zeros((1, TEXTS), jnp.float32))
-    for i in (0, 2):
-        parts = []
-        for u in range(2):
-            part, total = delta_part(c * N + order(0, i + u), total)
-            parts.append(part)
+    total = jnp.zeros((1, TEXTS), jnp.float32)
+    for i in range(2):
+        total = sib_part(i, total)
+    for i in range(2):
+        sib_copy(order(0, i)).start()
+    for i in range(2, N):
+        total = sib_part(i, total)
+
+    def image_emit(i, parts):
         for u in range(2):
             j = order(0, i + u)
             sib_copy(j).wait_recv()
             emit(0, i + u, parts[u] + stage_c[pair(j), :].astype(jnp.float32))
 
-    def text_part(i):
-        return lax.dot_general(
-            delta[:, pair(order(1, i))], img[...], (((0,), (0,)), ((), ())), preferred_element_type=jnp.float32
-        )
-
-    for i in (0, 2):
-        parts = [text_part(i), text_part(i + 1)]
-        for u in range(2):
+    def text_emit(i, count):
+        parts = [
+            lax.dot_general(
+                delta[:, pair(order(1, i + u))], img[...], (((0,), (0,)), ((), ())),
+                preferred_element_type=jnp.float32,
+            )
+            for u in range(count)
+        ]
+        for u in range(count):
             emit(1, i + u, parts[u])
 
+    parts = []
+    for i in range(2):
+        low, total = delta_part(c * N + order(0, i), total)
+        parts.append(image_part(low))
+    for i in range(2, N):
+        total = delta_part(c * N + order(0, i), total)[1]
+    for i in range(2, N):
+        sib_copy(order(0, i)).start()
+    image_emit(0, parts)
     sums[0, c] = jnp.where(lane == 1, jnp.sum(total, axis=1, keepdims=True), jnp.zeros((8, R), jnp.float32))
     eye = lax.broadcasted_iota(jnp.int32, (R, R), 0) == lax.broadcasted_iota(jnp.int32, (R, R), 1)
 
@@ -363,6 +387,15 @@
     lax.fori_loop(0, N * N, loss_step, 0)
     sum_go(0, c, [sib])
 
+    text_emit(0, 1)
+    text_emit(1, 1)
+    sum_take(0, 1 - c)
+    sums[1, ime] = sums[0, 0] + sums[0, 1]
+    sum_go(1, ime, same_i)
+    image_emit(2, [image_part(delta[pair(c * N + order(0, i)), :]) for i in range(2, N)])
+    text_emit(2, 2)
+
+
     def h0_sum(m, i):
         b = pair_me[m] if i else 1 - pair_me[m]
         acc = own0[m, i, ring_me[m] % 2]
@@ -390,15 +423,6 @@
 
     for v in far_blocks(0):
         second1(0, v)
-    second0(0)
-    sum_take(0, 1 - c)
-    sums[1, ime] = sums[0, 0] + sums[0, 1]
-    sum_go(1, ime, same_i)
-    for v in far_blocks(1):
-        second1(1, v)
-    second1(0, twin(0))
-    second0(1)
-    second1(1, twin(1))
     for t in others(yb, x):
         sum_take(1, t)
     acc = sums[1, 0]
@@ -406,6 +430,12 @@
         acc = acc + sums[1, v]
     sums[2, tme] = acc
     sum_go(2, tme, same_t)
+    second0(0)
+    for v in far_blocks(1):
+        second1(1, v)
+    second1(0, twin(0))
+    second0(1)
+    second1(1, twin(1))
     for m in range(2):
         fin[m, 0] = h0_sum(m, 1)
         fin[m, 1] = h1_sum(m, ring_me[m])

time: 70.8 us -> 66.5 us (0.939)
  Pallas kernels: 62.6 us -> 58.4 us
    pallas_call x1, Pallas kernels: 62.6 us -> 58.4 us  [local(): pl.pallas_call(kernel, out_shape=(jax.ShapeDtypeStruct((R, E), f32), jax....]
where the time goes in v5:
time: 66.5 us; the launch traced here: 65.8 us
  Pallas kernels  58.4 us (88%)
  between operations  4.81 us (7%)
  local copies, waits for them, and re-layouts  2.57 us (4%)
    pallas_call x1, Pallas kernels, local(): pl.pallas_call(kernel, out_shape=(jax.ShapeDtypeStruct((R, E), f32), jax....  58.4 us
    unnamed x4, local copies, waits for them, and re-layouts  2.57 us

profile of v5, /device:TPU:0, one launch (start us, length us, event | category | flops | bytes accessed | tf_op | source)
XLA Modules:
  0.0 65.8 jit_solution(12187572930167364622)
XLA Ops:
  1.3 58.4 %shard_map.66 = (f32[128,768]{1,0:T(8,128)}, f32[128,768]{1,0:T(8,128)}, f32[1]{0:T(128)}, f32[1]{0:T(128)}) custom-call(bf16[128,768]{1,0:T(8,128)(2,1)} %img_ref.1, bf16[128,768]{1,0:T(8,128)(2,1)} %txt_ref.1, f32[1]{0:T(128)} %bitcast.3.scale_ref), custom_call_target="tpu_custom_call" | custom-call | tf_op jit(solution)/shard_map/pallas_call | solution.py:484
  59.7 0.0 copy-start
  59.7 1.8 %copy.12 = f32[128,768]{1,0:T(8,128)} copy(f32[128,768]{1,0:T(8,128)} %get-tuple-element.16) | data formatting | bytes 786432
  61.5 0.0 copy-done
  61.5 0.7 %copy.13 = f32[128,768]{1,0:T(8,128)} copy(f32[128,768]{1,0:T(8,128)S(1)} %copy-done) | data formatting | bytes 786432
Async XLA Ops:
  59.7 1.8 %copy-start = (f32[128,768]{1,0:T(8,128)S(1)}, f32[128,768]{1,0:T(8,128)}, u32[]{:S(2)}) copy-start(f32[128,768]{1,0:T(8,128)} %get-tuple-element.17) | copy-start | bytes 1179652

commit v6 on v5

--- a/solution.py
+++ b/solution.py
@@ -42,7 +42,7 @@
 
 
 def kernel(
-    img_ref, txt_ref, scale_ref, gi_ref, gt_ref, loss_ref, gs_ref,
+    img_ref, txt_ref, scale_ref, sum_ref, whole_ref,
     img, txt, logit, delta, stage_s, stage_c, stage_i, stage_t,
     own0, own1, fin, a0, a1, sb, b0, b1,
     rowl, rowp, rowx, coll, colz, sums,
@@ -441,26 +441,23 @@
         fin[m, 1] = h1_sum(m, ring_me[m])
 
     factor = scale * (1.0 / (2.0 * TEXTS * N * N))
-    sources, results = (img_ref, txt_ref), (gi_ref, gt_ref)
     for m in range(2):
         take(b0.at[m], pb0_r.at[m])
         acc = fin[m, 0] + b0[m].astype(jnp.float32)
-        results[m][:H, :] = project(sources[m][:H, :], factor * acc)
+        sum_ref[m, :H, :] = factor * acc
         acc = fin[m, 1]
         for d in range(1, N):
             s = turn(ring_me[m], d)
             take(b1.at[m, s], pb1_r.at[m, s])
             acc = acc + b1[m, s].astype(jnp.float32)
-        results[m][H:, :] = project(sources[m][H:, :], factor * acc)
+        sum_ref[m, H:, :] = factor * acc
     for t in others(yo, z):
         sum_take(2, t)
     whole = sums[2, 0]
     for v in range(1, 2 * N):
         whole = whole + sums[2, v]
     whole = whole * (LN2 / (2.0 * TEXTS * N * N))
-    top = lax.broadcasted_iota(jnp.int32, (8, R), 0) == 0
-    loss_ref[0] = jnp.sum(jnp.where(jnp.logical_and(top, lane == 0), whole, 0.0))
-    gs_ref[0] = jnp.sum(jnp.where(jnp.logical_and(top, lane == 1), whole, 0.0))
+    whole_ref[...] = whole
 
     for copy in started:
         copy.wait_send()
@@ -476,21 +473,26 @@
         sib_copy(j).wait_send()
 
 
+def finish(img_ref, txt_ref, sum_ref, whole_ref, gi_ref, gt_ref, loss_ref, gs_ref):
+    gi_ref[...] = project(img_ref[...], sum_ref[0])
+    gt_ref[...] = project(txt_ref[...], sum_ref[1])
+    whole = whole_ref[...]
+    lane = lax.broadcasted_iota(jnp.int32, (8, R), 1)
+    top = lax.broadcasted_iota(jnp.int32, (8, R), 0) == 0
+    loss_ref[0] = jnp.sum(jnp.where(jnp.logical_and(top, lane == 0), whole, 0.0))
+    gs_ref[0] = jnp.sum(jnp.where(jnp.logical_and(top, lane == 1), whole, 0.0))
+
+
 def local(images, texts, log_scale):
     f32, bf16 = jnp.float32, jnp.bfloat16
     dma = pltpu.SemaphoreType.DMA
     vmem = pl.BlockSpec(memory_space=pltpu.VMEM)
     smem = pl.BlockSpec(memory_space=pltpu.SMEM)
-    gi, gt, loss, gs = pl.pallas_call(
+    sums, whole = pl.pallas_call(
         kernel,
-        out_shape=(
-            jax.ShapeDtypeStruct((R, E), f32),
-            jax.ShapeDtypeStruct((R, E), f32),
-            jax.ShapeDtypeStruct((1,), f32),
-            jax.ShapeDtypeStruct((1,), f32),
-        ),
+        out_shape=(jax.ShapeDtypeStruct((2, R, E), f32), jax.ShapeDtypeStruct((8, R), f32)),
         in_specs=[vmem, vmem, smem],
-        out_specs=(vmem, vmem, smem, smem),
+        out_specs=(vmem, vmem),
         scratch_shapes=[
             pltpu.VMEM((IMAGES, E), bf16),
             pltpu.VMEM((TEXTS, E), bf16),
@@ -528,6 +530,17 @@
             collective_id=0, has_side_effects=True, vmem_limit_bytes=56 * 1024 * 1024
         ),
     )(images, texts, log_scale.reshape(1))
+    gi, gt, loss, gs = pl.pallas_call(
+        finish,
+        out_shape=(
+            jax.ShapeDtypeStruct((R, E), f32),
+            jax.ShapeDtypeStruct((R, E), f32),
+            jax.ShapeDtypeStruct((1,), f32),
+            jax.ShapeDtypeStruct((1,), f32),
+        ),
+        in_specs=[vmem, vmem, vmem, vmem],
+        out_specs=(vmem, vmem, smem, smem),
+    )(images, texts, sums, whole)
     return gi, gt, loss.reshape(()), gs.reshape(())
 
 

time: 66.5 us -> 62.7 us (0.943)
  between operations: 4.81 us -> 1.45 us
  local copies, waits for them, and re-layouts: 2.57 us -> 0 us
  Pallas kernels: 58.4 us -> 60.6 us
    unnamed x4 -> x0, local copies, waits for them, and re-layouts: 2.57 us -> none
    pallas_call x1 -> x2, Pallas kernels: 58.4 us -> 60.6 us  [the longest x1 58.1 us: local(): pl.pallas_call(kernel, out_shape=(jax.ShapeDtypeStruct((2, R, E), f32), j...]
where the time goes in v6:
time: 62.7 us; the launch traced here: 62 us
  Pallas kernels  60.6 us (97%)
  between operations  1.45 us (2%)
    pallas_call x1, Pallas kernels, local(): pl.pallas_call(kernel, out_shape=(jax.ShapeDtypeStruct((2, R, E), f32), j...  58.1 us
    pallas_call x1, Pallas kernels, local(): pl.pallas_call(finish, out_shape=(jax.ShapeDtypeStruct((R, E), f32), jax....  2.46 us

profile of v6, /device:TPU:0, one launch (start us, length us, event | category | flops | bytes accessed | tf_op | source)
XLA Modules:
  0.0 62.0 jit_solution(615619749177681488)
XLA Ops:
  1.3 58.1 %shard_map.66 = (f32[2,128,768]{2,1,0:T(8,128)}, f32[8,128]{1,0:T(8,128)}) custom-call(bf16[128,768]{1,0:T(8,128)(2,1)} %img_ref.3, bf16[128,768]{1,0:T(8,128)(2,1)} %txt_ref.3, f32[1]{0:T(128)} %bitcast.3.scale_ref), custom_call_target="tpu_custom_call" | custom-call | tf_op jit(solution)/shard_map/pallas_call | solution.py:491
  59.4 2.5 %shard_map.67 = (f32[128,768]{1,0:T(8,128)}, f32[128,768]{1,0:T(8,128)}, f32[1]{0:T(128)}, f32[1]{0:T(128)}) custom-call(bf16[128,768]{1,0:T(8,128)(2,1)} %img_ref.3, bf16[128,768]{1,0:T(8,128)(2,1)} %txt_ref.3, f32[2,128,768]{2,1,0:T(8,128)} %get-tuple-element.10.sum_ref, f32[8,128]{1,0:T(8,128)} %get-tuple-element.11.whole_ref), custom_call_target="tpu_custom_call" | custom-call | tf_op jit(solution)/shard_map/pallas_call | solution.py:533

commit v7 on v6

--- a/solution.py
+++ b/solution.py
@@ -430,12 +430,12 @@
         acc = acc + sums[1, v]
     sums[2, tme] = acc
     sum_go(2, tme, same_t)
-    second0(0)
     for v in far_blocks(1):
         second1(1, v)
     second1(0, twin(0))
+    second0(0)
+    second1(1, twin(1))
     second0(1)
-    second1(1, twin(1))
     for m in range(2):
         fin[m, 0] = h0_sum(m, 1)
         fin[m, 1] = h1_sum(m, ring_me[m])

time: 62.7 us -> 62.7 us (level)
  no operation moved by 1% of the time
where the time goes in v7:
time: 62.7 us; the launch traced here: 62 us
  Pallas kernels  60.6 us (97%)
  between operations  1.45 us (2%)
    pallas_call x1, Pallas kernels, local(): pl.pallas_call(kernel, out_shape=(jax.ShapeDtypeStruct((2, R, E), f32), j...  58.1 us
    pallas_call x1, Pallas kernels, local(): pl.pallas_call(finish, out_shape=(jax.ShapeDtypeStruct((R, E), f32), jax....  2.46 us

profile of v7, /device:TPU:0, one launch (start us, length us, event | category | flops | bytes accessed | tf_op | source)
XLA Modules:
  0.0 62.0 jit_solution(16163280180793207492)
XLA Ops:
  1.3 58.1 %shard_map.66 = (f32[2,128,768]{2,1,0:T(8,128)}, f32[8,128]{1,0:T(8,128)}) custom-call(bf16[128,768]{1,0:T(8,128)(2,1)} %img_ref.3, bf16[128,768]{1,0:T(8,128)(2,1)} %txt_ref.3, f32[1]{0:T(128)} %bitcast.3.scale_ref), custom_call_target="tpu_custom_call" | custom-call | tf_op jit(solution)/shard_map/pallas_call | solution.py:491
  59.4 2.5 %shard_map.67 = (f32[128,768]{1,0:T(8,128)}, f32[128,768]{1,0:T(8,128)}, f32[1]{0:T(128)}, f32[1]{0:T(128)}) custom-call(bf16[128,768]{1,0:T(8,128)(2,1)} %img_ref.3, bf16[128,768]{1,0:T(8,128)(2,1)} %txt_ref.3, f32[2,128,768]{2,1,0:T(8,128)} %get-tuple-element.10.sum_ref, f32[8,128]{1,0:T(8,128)} %get-tuple-element.11.whole_ref), custom_call_target="tpu_custom_call" | custom-call | tf_op jit(solution)/shard_map/pallas_call | solution.py:533
